TPU v7x, 32 devices: a whole 2x2x4 slice. The times are simulated.
32 devices in a mesh: wide: 8 (over z, y), narrow: 4 (over x, core).
Axes of the slice: x: 2, y: 2, z: 4, core: 2. Of those that a mesh axis runs over, the one named last changes fastest.
Arguments:
- amplitudes: bfloat16 [512, 8, 4096], P('narrow', 'wide'), may hold values from -6 to 6
- integrals: bfloat16 [8, 2, 4096, 4096], P('wide', None, None, 'narrow'), may hold values from -0.09375 to 0.09375
- targets: int32 [8, 2], replicated, may hold values from 0 to 7, as said below
- counts: int32 [8], replicated, may hold values from 1 to 2, as said below
Outputs:
- residual: float32 [512, 8, 4096], P('wide', None, 'narrow')
Inputs may be any that keep to these rules, and one draw needn't show every extreme that they name: `targets`: the 2 entries of one row are different pair tiles. `counts`: every panel holds at least one block.
All inputs are finite; a program needn't handle non-finite values.
Results may differ from a plain program's by a relative error of at most 0.0003.
Values may be sent and summed in bfloat16 or wider, within the bound.
No kernel may reach another device: no remote copies, remote signals or barrier semaphores. Data moves between devices by JAX's collectives and lax.ppermute only.
A program may use at most 64 MiB of HBM per device.

v0:
```python
import jax
import jax.numpy as jnp
from jax import lax
from jax.sharding import PartitionSpec as P


def on_device(amplitudes, integrals, targets, counts):
    wide_count = lax.axis_size("wide")
    panel_index = lax.axis_index("wide")
    slot_total = integrals.shape[1]
    pair_total = targets.shape[0]
    col_width = integrals.shape[3]
    own_rows = amplitudes.reshape(amplitudes.shape[0], amplitudes.shape[2])
    own_live = lax.dynamic_index_in_dim(counts, panel_index, 0, keepdims=False)
    gathered = lax.all_gather(own_rows, "narrow", axis=0, tiled=True)
    products = []
    for slot_index in range(slot_total):
        product = jnp.dot(gathered, integrals[0, slot_index], preferred_element_type=jnp.float32)
        products.append(jnp.where(slot_index < own_live, product, 0.0))
    partial_value = jnp.stack(products, axis=1)
    slot_ids = jnp.arange(slot_total, dtype=jnp.int32)
    tile_ids = jnp.arange(pair_total, dtype=jnp.int32)
    live_slots = slot_ids[None, :] < counts[:, None]
    selector = ((targets[:, :, None] == tile_ids[None, None, :]) & live_slots[:, :, None]).astype(
        jnp.float32
    )
    received = lax.all_to_all(partial_value, "wide", split_axis=0, concat_axis=0, tiled=True)
    shaped = received.reshape(wide_count, -1, slot_total, col_width)
    residual = jnp.einsum("nrsc,nsp->rpc", shaped, selector, precision=lax.Precision.HIGHEST)
    return residual


def solution(mesh):
    in_specs = (P("narrow", "wide", None), P("wide", None, None, "narrow"), P(), P())
    out_specs = P("wide", None, "narrow")
    return jax.shard_map(
        on_device, mesh=mesh, in_specs=in_specs, out_specs=out_specs, check_vma=False
    )
```

profile of v0, /device:TPU:0, one launch (start us, length us, event | category | flops | bytes accessed | tf_op | source)
XLA Modules:
  0.0 180.2 jit_solution(8512462039592607336)
XLA Ops:
  6.5 0.0 all-gather.3.cloned.1.call-start
  6.5 0.7 all-gather.3.cloned.1.call-update
  7.3 1.2 dynamic_slice.4
  9.8 36.3 %all-gather.3.cloned.1.call-done = bf16[512,1,4096]{2,0,1:T(8,128)(2,1)} async-done(((bf16[128,1,4096]{2,0,1:T(8,128)(2,1)}), bf16[512,1,4096]{2,0,1:T(8,128)(2,1)}) %all-gather.3.cloned.1.call-update) | async-done | bytes 4194320 | tf_op jit(solution)/shard_map/all_gather | solution.py:15
  46.1 0.0 copy-start.1
  46.1 0.0 copy-start.2
  46.1 8.3 %select_bitcast_fusion.1 = f32[512,1,1024]{2,0,1:T(8,128)S(1)} fusion(bf16[1,2,4096,1024]{3,2,1,0:T(8,128)(2,1)} %param.5, bf16[512,1,4096]{2,0,1:T(8,128)(2,1)} %all-gather.3.cloned.1.call-done, pred[]{:T(512)} %bitcast.1), kind=kOutput, calls=%fused_computation.12 | convolution fusion | flops 4295491584 | bytes 14680576 | tf_op jit(solution)/shard_map/dot_general | solution.py:18
  54.4 1.1 copy-done.1
  55.5 1.2 copy-done.2
  56.7 4.5 %select_bitcast_fusion = f32[512,1,1024]{2,0,1:T(8,128)S(1)} fusion(bf16[1,2,4096,1024]{3,2,1,0:T(8,128)(2,1)S(1)} %copy-done.1, bf16[512,1,4096]{2,0,1:T(8,128)(2,1)S(1)} %copy-done.2, pred[]{:T(512)} %bitcast.5), kind=kOutput, calls=%fused_computation.11 | convolution fusion | flops 4295491584 | bytes 14680065 | tf_op jit(solution)/shard_map/dot_general | solution.py:18
  61.3 0.3 pad_maximum_fusion
  61.6 5.2 %copy.7 = f32[512,2,1024]{2,1,0:T(2,128)} copy(f32[512,2,1024]{2,0,1:T(8,128)S(1)} %pad_maximum_fusion) | data formatting | bytes 8388608 | tf_op jit(solution)/shard_map/stack | solution.py:20
  66.8 0.0 copy-start.3
  66.8 0.0 copy-start
  66.8 5.6 %all-to-all-start = ((f32[512,2,1024]{2,1,0:T(2,128)}), f32[512,2,1024]{2,1,0:T(2,128)}, u32[]{:S(2)}, u32[]{:S(2)}) async-start(f32[512,2,1024]{2,1,0:T(2,128)} %copy.7), calls=%async_computation | async-start | bytes 8388608 | tf_op jit(solution)/shard_map/all_to_all | solution.py:27
  72.5 0.0 copy-done.3
  72.5 93.7 %all-to-all-done = f32[512,2,1024]{2,1,0:T(2,128)} async-done(((f32[512,2,1024]{2,1,0:T(2,128)}), f32[512,2,1024]{2,1,0:T(2,128)}, u32[]{:S(2)}, u32[]{:S(2)}) %all-to-all-start) | async-done | bytes 4194336 | tf_op jit(solution)/shard_map/all_to_all | solution.py:27
  166.2 0.0 copy-done
  166.2 7.2 %fusion.10 = f32[64,8,1024]{2,1,0:T(8,128)} fusion(f32[8,64,2,1024]{3,2,1,0:T(2,128)} %bitcast.8, s32[8,2]{0,1:T(2,128)S(1)} %copy-done, pred[8,2]{0,1:T(4,128)(4,1)S(1)} %iota_compare_fusion.1), kind=kOutput, calls=%fused_computation.13 | convolution fusion | flops 100663552 | bytes 6291536 | tf_op jit(solution)/shard_map/nrsc,nsp->rpc/dot_general | solution.py:29
  (1 shorter events, 0.0 us)
Async XLA Ops:
  6.5 39.6 %all-gather.3.cloned.1.call-start = ((), (), s32[]{:S(2)}) async-start(), calls=%async_computation.1 | async-start | bytes 5242880 | tf_op jit(solution)/shard_map/all_gather | solution.py:15
  46.1 9.4 %copy-start.1 = (bf16[1,2,4096,1024]{3,2,1,0:T(8,128)(2,1)S(1)}, bf16[1,2,4096,1024]{3,2,1,0:T(8,128)(2,1)}, u32[]{:S(2)}) copy-start(bf16[1,2,4096,1024]{3,2,1,0:T(8,128)(2,1)} %param.5) | copy-start | bytes 50331652
  46.1 10.6 %copy-start.2 = (bf16[512,1,4096]{2,0,1:T(8,128)(2,1)S(1)}, bf16[512,1,4096]{2,0,1:T(8,128)(2,1)}, u32[]{:S(2)}) copy-start(bf16[512,1,4096]{2,0,1:T(8,128)(2,1)} %all-gather.3.cloned.1.call-done) | copy-start | bytes 12582916
  66.8 5.7 %copy-start.3 = (s32[8]{0:T(128)S(1)}, s32[8]{0:T(128)}, u32[]{:S(2)}) copy-start(s32[8]{0:T(128)} %param.7) | copy-start | bytes 100
  66.8 99.3 %copy-start = (s32[8,2]{0,1:T(2,128)S(1)}, s32[8,2]{0,1:T(2,128)}, u32[]{:S(2)}) copy-start(s32[8,2]{0,1:T(2,128)} %param.6) | copy-start | bytes 196
  66.8 99.3 %all-to-all-start = ((f32[512,2,1024]{2,1,0:T(2,128)}), f32[512,2,1024]{2,1,0:T(2,128)}, u32[]{:S(2)}, u32[]{:S(2)}) async-start(f32[512,2,1024]{2,1,0:T(2,128)} %copy.7), calls=%async_computation | async-start | bytes 8388608 | tf_op jit(solution)/shard_map/all_to_all | solution.py:27
Sparse Core Ops, SparseCore 0:
  8.9 37.1 all-gather.2
where the time goes:
time: 181 us; the launch traced here: 180 us
  waiting for transfers between devices  131 us (72%)
  matrix products  20 us (11%)
  between operations  14.7 us (8%)
  local copies, waits for them, and re-layouts  8.79 us (5%)
  starting transfers between devices  5.65 us (3%)
    all_to_all x1, waiting for transfers between devices, on_device(): lax.all_to_all(partial_value, 'wide', split_axis=0, concat_axis=0, tiled=...  93.7 us
    all_gather x1, waiting for transfers between devices, on_device(): gathered = lax.all_gather(own_rows, 'narrow', axis=0, tiled=True)  36.3 us
    dot_general x2, matrix products, on_device(): jnp.dot(gathered, integrals[0, slot_index], preferred_element_type=jnp.fl...  12.8 us
    dot_general x1, matrix products, on_device(): jnp.einsum('nrsc,nsp->rpc', shaped, selector, precision=lax.Precision.HIG...  7.23 us
    all_to_all x1, starting transfers between devices, on_device(): lax.all_to_all(partial_value, 'wide', split_axis=0, concat_axis=0, tiled=...  5.65 us
    another operation x1, local copies, waits for them, and re-layouts, on_device(): partial_value = jnp.stack(products, axis=1)  5.22 us
  transfers between devices with their start and end apart: 2, of which 2 were waited for; matrix products, arithmetic and copies ran while one was open for 1% of the time, Pallas kernels for 0%

commit v1 on v0

v1 whole, which is shorter than its diff:
```python
import functools

import jax
import jax.numpy as jnp
from jax import lax
from jax.experimental import pallas as pl
from jax.experimental.pallas import tpu as pltpu
from jax.sharding import PartitionSpec as P

MIB = 1 << 20
TOP = 32766.0
MANT = 8192.0
MODES = ("direct", "direct")


def scale_code(peak):
    exponent = jnp.clip(jnp.floor(jnp.log2(jnp.maximum(peak, 1e-37))), -125.0, 125.0)
    mantissa = jnp.minimum(jnp.ceil(peak * jnp.exp2(-exponent) * MANT) + 1.0, 32000.0)
    return exponent, jnp.maximum(mantissa, 1.0)


def stage_kernel(source, kept, done):
    copy = pltpu.make_async_copy(source, kept, done)
    copy.start()
    copy.wait()


def staged(integrals):
    return pl.pallas_call(
        stage_kernel,
        out_shape=pltpu.VMEM(integrals.shape, integrals.dtype),
        in_specs=[pl.BlockSpec(memory_space=pltpu.HBM)],
        out_specs=pl.BlockSpec(memory_space=pltpu.VMEM),
        scratch_shapes=[pltpu.SemaphoreType.DMA],
        compiler_params=pltpu.CompilerParams(vmem_limit_bytes=40 * MIB),
        name="staged_integrals",
    )(integrals)


def pick_kernel(source, *refs):
    refs[-1][...] = source[...]


def picked(own, start, rows, after):
    share, _, depth = own.shape
    return pl.pallas_call(
        pick_kernel,
        out_shape=jax.ShapeDtypeStruct((share, rows, depth), own.dtype),
        grid=(1,),
        in_specs=[pl.BlockSpec((share, rows, depth), lambda i: (0, start // rows, 0))]
        + [pl.BlockSpec(memory_space=pl.ANY)] * len(after),
        out_specs=pl.BlockSpec((share, rows, depth), lambda i: (0, 0, 0)),
        compiler_params=pltpu.CompilerParams(vmem_limit_bytes=8 * MIB),
        name="picked_rows",
    )(own, *after)


def product_kernel(slots, wide, narrow, share, rows, joint, ids, *refs):
    pieces, block = refs[:narrow], refs[narrow]
    outs = refs[narrow + 1 : -3]
    left, total, codes = refs[-3:]
    me, mine = ids[0], ids[1]
    cols = block.shape[3]
    groups, lanes = rows // 16, cols // 128
    tiles = slots * groups * lanes + 1
    for k in range(narrow):
        for sub in range(share):
            place = ((mine ^ k) * share + sub) ^ me
            left[pl.ds(pl.multiple_of(place * rows, rows), rows), :] = pieces[k][sub]
    codes[...] = jnp.zeros_like(codes)
    lane = lax.broadcasted_iota(jnp.int32, (16, 128), 1)

    def one_slot(slot, carry):
        for n in range(cols // 256):
            span = slice(n * 256, n * 256 + 256)
            total[:, span] = jnp.dot(left[...], block[0, slot, :, span], preferred_element_type=jnp.float32)
        for s in range(wide):
            for g in range(groups):
                value = total[s * rows + g * 16 : s * rows + g * 16 + 16, :]
                peak = jnp.max(jnp.abs(value), axis=1, keepdims=True)
                exponent, mantissa = scale_code(peak)
                value = value * jnp.exp2(-exponent) * (TOP * MANT / mantissa)
                value = jnp.round(value).astype(jnp.int32).astype(jnp.int16)
                at = (s % joint) * tiles + (slot * groups + g) * lanes
                for t in range(lanes):
                    outs[s // joint][at + t] = value[:, t * 128 : t * 128 + 128]
                spot = (slot * groups + g) * 2
                code = jnp.where(lane == spot, exponent.astype(jnp.int32), codes[s])
                codes[s] = jnp.where(lane == spot + 1, mantissa.astype(jnp.int32), code)
        return carry

    lax.fori_loop(0, slots, one_slot, 0)
    for s in range(wide):
        outs[s // joint][(s % joint) * tiles + tiles - 1] = codes[s].astype(jnp.int16)


def products(ids, pieces, integrals, wide, joint):
    _, slots, depth, cols = integrals.shape
    narrow = len(pieces)
    share, rows, _ = pieces[0].shape
    tiles = slots * (rows // 16) * (cols // 128) + 1
    vmem = pl.BlockSpec(memory_space=pltpu.VMEM)
    return pl.pallas_call(
        functools.partial(product_kernel, slots, wide, narrow, share, rows, joint),
        out_shape=[jax.ShapeDtypeStruct((joint * tiles, 16, 128), jnp.int16)] * (wide // joint),
        in_specs=[pl.BlockSpec(memory_space=pltpu.SMEM)] + [vmem] * (narrow + 1),
        out_specs=[vmem] * (wide // joint),
        scratch_shapes=[
            pltpu.VMEM((wide * rows, depth), jnp.bfloat16),
            pltpu.VMEM((wide * rows, cols), jnp.float32),
            pltpu.VMEM((wide, 16, 128), jnp.int32),
        ],
        compiler_params=pltpu.CompilerParams(vmem_limit_bytes=16 * MIB),
        cost_estimate=pl.CostEstimate(
            flops=16 * slots * wide * rows * depth * cols,
            bytes_accessed=2 * wide * rows * depth,
            transcendentals=0,
        ),
        name="products",
    )(ids, *pieces, integrals)


def sum_kernel(slots, plan, rows, cols, ids, targets, counts, *refs):
    out, total = refs[-2:]
    me = ids[0]
    groups, lanes = rows // 16, cols // 128
    tiles = slots * groups * lanes + 1
    total[...] = jnp.zeros_like(total)
    lane = lax.broadcasted_iota(jnp.int32, (16, 128), 1)
    for index, bits, at in plan:
        panel = me ^ bits
        codes = refs[index][at + tiles - 1].astype(jnp.int32)
        for j in range(slots):

            @pl.when(j < counts[panel])
            def add():
                tile = targets[panel * slots + j]
                for g in range(groups):
                    spot = (j * groups + g) * 2
                    exponent = jnp.sum(jnp.where(lane == spot, codes, 0).astype(jnp.float32), axis=1, keepdims=True)
                    mantissa = jnp.sum(jnp.where(lane == spot + 1, codes, 0).astype(jnp.float32), axis=1, keepdims=True)
                    scale = jnp.exp2(exponent) * (mantissa * (1.0 / (TOP * MANT)))
                    for t in range(lanes):
                        value = refs[index][at + (j * groups + g) * lanes + t].astype(jnp.int32).astype(jnp.float32)
                        total[tile, g * 16 : g * 16 + 16, t * 128 : t * 128 + 128] += value * scale
    for g in range(rows // 8):
        for t in range(lanes):
            span = slice(t * 128, t * 128 + 128)
            out[g * 8 : g * 8 + 8, :, span] = jnp.swapaxes(total[:, g * 8 : g * 8 + 8, span], 0, 1)


def summed(ids, targets, counts, given, plan, held, start, rows, cols, height):
    pairs, slots = targets.shape
    extra = [] if held is None else [held]
    return pl.pallas_call(
        functools.partial(sum_kernel, slots, plan, rows, cols),
        out_shape=jax.ShapeDtypeStruct((height, pairs, cols), jnp.float32),
        grid_spec=pltpu.PrefetchScalarGridSpec(
            num_scalar_prefetch=3,
            grid=(1,),
            in_specs=[pl.BlockSpec(g.shape, lambda i, *_: (0, 0, 0)) for g in given]
            + [pl.BlockSpec(memory_space=pl.ANY)] * len(extra),
            out_specs=pl.BlockSpec((rows, pairs, cols), lambda i, *_: (start // rows, 0, 0)),
            scratch_shapes=[pltpu.VMEM((pairs, rows, cols), jnp.float32)],
        ),
        input_output_aliases={3 + len(given): 0} if extra else {},
        compiler_params=pltpu.CompilerParams(vmem_limit_bytes=32 * MIB),
        cost_estimate=pl.CostEstimate(
            flops=4 * pairs * slots * rows * cols,
            bytes_accessed=2 * pairs * slots * rows * cols + 4 * pairs * rows * cols,
            transcendentals=0,
        ),
        name="tile_sums",
    )(ids, targets.reshape(-1), counts, *given, *extra)


def on_device(amplitudes, integrals, targets, counts):
    wide, narrow = lax.axis_size("wide"), lax.axis_size("narrow")
    me, mine = lax.axis_index("wide"), lax.axis_index("narrow")
    ids = jnp.stack([me, mine]).astype(jnp.int32)
    depth, cols = integrals.shape[2], integrals.shape[3]
    share = wide // narrow
    height = amplitudes.shape[0] // share
    own = amplitudes.reshape(share, height, depth)
    parts = [16] * (height // 16) if height < 64 else [32, height - 32]

    def across(array, axis, size, bits):
        return lax.ppermute(array, axis, [(i, i ^ bits) for i in range(size)])

    starts = [sum(parts[:i]) for i in range(len(parts))]
    kept = staged(integrals)
    beside = across(own, "narrow", narrow, 1)
    received, arrivals, after, ready = [], [], [], [kept]
    for start, rows, mode in zip(starts, parts, MODES):
        chunk = picked(own, start, rows, after)
        far = [across(chunk, "narrow", narrow, k) for k in range(2, narrow, 2)]
        after = far[-1:]
        far = [picked(c, 0, rows, ready) if ready else c for c in far]
        odd = [across(c, "narrow", narrow, 1) for c in far]
        pieces = [chunk, beside[:, start : start + rows]] + [piece for pair in zip(far, odd) for piece in pair]
        joint = 2 if mode == "relay" else 1
        sent = products(ids, pieces, kept, wide, joint)
        order = range(wide // joint - 1, 0, -1)
        given = [across(sent[k], "wide", wide, joint * k) for k in order] + [sent[0]]
        plan = [(i, joint * k, 0) for i, k in enumerate([*order, 0])]
        arrivals.append(given[:-1])
        if mode == "relay":
            size = given[0].shape[0] // 2
            passed = across(jnp.concatenate([g[size:] for g in given]), "wide", wide, 1)
            plan += [(len(given), (2 * k) ^ 1, i * size) for i, k in enumerate([*order, 0])]
            given.append(passed)
        received.append((given, tuple(plan)))
        ready = [sent[0]]
    held = None
    for (given, plan), start, rows in zip(received, starts, parts):
        held = summed(ids, targets, counts, given, plan, held, start, rows, cols, height)
    return held


def solution(mesh):
    in_specs = (P("narrow", "wide", None), P("wide", None, None, "narrow"), P(), P())
    out_specs = P("wide", None, "narrow")
    return jax.shard_map(
        on_device, mesh=mesh, in_specs=in_specs, out_specs=out_specs, check_vma=False
    )
```

time: 181 us -> 86.8 us (0.48)
  waiting for transfers between devices: 131 us -> 20.6 us
  starting transfers between devices: 5.65 us -> 40.9 us
  Pallas kernels: 0 us -> 23.7 us
  matrix products: 20 us -> 0 us
  between operations: 14.7 us -> 0.11 us
  local copies, waits for them, and re-layouts: 8.79 us -> 1.47 us
    all_to_all x1 -> x0, waiting for transfers between devices: 93.7 us -> none  [on_device(): lax.all_to_all(partial_value, 'wide', split_axis=0, concat_axis=0, tiled=...]
    ppermute x0 -> x19, starting transfers between devices: none -> 40.9 us  [across(): return lax.ppermute(array, axis, [(i, i ^ bits) for i in range(size)])]
    all_gather x1 -> x0, waiting for transfers between devices: 36.3 us -> none  [on_device(): gathered = lax.all_gather(own_rows, 'narrow', axis=0, tiled=True)]
    pallas_call x0 -> x9, Pallas kernels: none -> 23.7 us  [the longest x2 11.7 us: products(): pl.pallas_call(functools.partial(product_kernel, slots, wide, narrow, sha...]
    ppermute x0 -> x19, waiting for transfers between devices: none -> 20.6 us  [across(): return lax.ppermute(array, axis, [(i, i ^ bits) for i in range(size)])]
    dot_general x3 -> x0, matrix products: 20 us -> none  [the longest x2 12.8 us: on_device(): jnp.dot(gathered, integrals[0, slot_index], preferred_element_type=jnp.fl...]
    all_to_all x1 -> x0, starting transfers between devices: 5.65 us -> none  [on_device(): lax.all_to_all(partial_value, 'wide', split_axis=0, concat_axis=0, tiled=...]
    another operation x1 -> x0, local copies, waits for them, and re-layouts: 5.22 us -> none  [on_device(): partial_value = jnp.stack(products, axis=1)]
  transfers between devices with their start and end apart: 2 -> 19, of which waited for: 2 -> 8; matrix products, arithmetic and copies ran while one was open for 1% -> 0% of each run, Pallas kernels for 0% -> 24%
where the time goes in v1:
time: 86.8 us
  starting transfers between devices  40.9 us (47%)
  Pallas kernels  23.7 us (27%)
  waiting for transfers between devices  20.6 us (24%)
  local copies, waits for them, and re-layouts  1.47 us (2%)
    ppermute x19, starting transfers between devices, across(): return lax.ppermute(array, axis, [(i, i ^ bits) for i in range(size)])  40.9 us
    ppermute x19, waiting for transfers between devices, across(): return lax.ppermute(array, axis, [(i, i ^ bits) for i in range(size)])  20.6 us
    pallas_call x2, Pallas kernels, products(): pl.pallas_call(functools.partial(product_kernel, slots, wide, narrow, sha...  11.7 us
    pallas_call x2, Pallas kernels, summed(): pl.pallas_call(functools.partial(sum_kernel, slots, plan, rows, cols), ou...  6 us
    pallas_call x1, Pallas kernels, staged(): pl.pallas_call(stage_kernel, out_shape=pltpu.VMEM(integrals.shape, integr...  5.87 us
  transfers between devices with their start and end apart: 19, of which 8 were waited for; matrix products, arithmetic and copies ran while one was open for 0% of the time, Pallas kernels for 24%

profile of v1, /device:TPU:0, one launch (start us, length us, event | category | flops | bytes accessed | tf_op | source)
XLA Modules:
  0.0 86.8 jit_solution(15512488772225629034)
XLA Ops:
  0.0 0.5 collective-permute-start.1
  0.5 1.2 %copy-done = bf16[128,1,4096]{2,0,1:T(8,128)(2,1)S(1)} copy-done((bf16[128,1,4096]{2,0,1:T(8,128)(2,1)S(1)}, bf16[128,1,4096]{2,0,1:T(8,128)(2,1)}, u32[]{:S(2)}) %copy-start) | copy-done | bytes 1048600
  1.7 2.6 %collective-permute-start = (bf16[2,32,4096]{2,1,0:T(8,128)(2,1)S(1)}, bf16[2,32,4096]{2,1,0:T(8,128)(2,1)S(1)}, u32[]{:S(2)}, u32[]{:S(2)}) collective-permute-start(bf16[2,32,4096]{2,1,0:T(8,128)(2,1)S(1)} %picked_rows.4.refs_0_), channel_id=1, source_target_pairs={{0,2},{1,3},{2,0},{3,1},{4,6},{5,7},{6,4},{7,5},{8,10},{9,11},{10,... | collective-permute-start | bytes 1572872 | tf_op jit(solution)/shard_map/ppermute | solution.py:188
  4.3 5.9 %staged_integrals.1.refs_0_.refs_4_ = bf16[1,2,4096,1024]{3,2,1,0:T(8,128)(2,1)S(1)} custom-call(bf16[1,2,4096,1024]{3,2,1,0:T(8,128)(2,1)} %source.1), custom_call_target="tpu_custom_call" | custom-call | tf_op jit(solution)/shard_map/staged_integrals/pallas_call | solution.py:29
  10.1 0.1 pad_add_fusion.ids
  10.2 6.6 %collective-permute-done.refs_0_.source = bf16[2,32,4096]{2,1,0:T(8,128)(2,1)S(1)} collective-permute-done((bf16[2,32,4096]{2,1,0:T(8,128)(2,1)S(1)}, bf16[2,32,4096]{2,1,0:T(8,128)(2,1)S(1)}, u32[]{:S(2)}, u32[]{:S(2)}) %collective-permute-start) | collective-permute-done | bytes 524320 | tf_op jit(solution)/shard_map/ppermute | solution.py:188
  16.9 1.8 %collective-permute-start.2 = (bf16[2,32,4096]{2,1,0:T(8,128)(2,1)S(1)}, bf16[2,32,4096]{2,1,0:T(8,128)(2,1)S(1)}, u32[]{:S(2)}, u32[]{:S(2)}) collective-permute-start(bf16[2,32,4096]{2,1,0:T(8,128)(2,1)S(1)} %picked_rows.5.refs_0_), channel_id=1, source_target_pairs={{0,2},{1,3},{2,0},{3,1},{4,6},{5,7},{6,4},{7,5},{8,10},{9,11},{10,... | collective-permute-start | bytes 1572872 | tf_op jit(solution)/shard_map/ppermute | solution.py:188
  18.9 1.8 %collective-permute-done.3.refs_3_ = bf16[2,32,4096]{2,1,0:T(8,128)(2,1)S(1)} collective-permute-done((bf16[2,32,4096]{2,1,0:T(8,128)(2,1)S(1)}, bf16[2,32,4096]{2,1,0:T(8,128)(2,1)S(1)}, u32[]{:S(2)}, u32[]{:S(2)}) %collective-permute-start.3) | collective-permute-done | bytes 524320 | tf_op jit(solution)/shard_map/ppermute | solution.py:188
  20.7 5.8 %products.2 = (s16[33,16,128]{2,1,0:T(8,128)(2,1)S(1)}, s16[33,16,128]{2,1,0:T(8,128)(2,1)S(1)}, s16[33,16,128]{2,1,0:T(8,128)(2,1)S(1)}, s16[33,16,128]{2,1,0:T...) custom-call(s32[2]{0:T(128)S(1)} %pad_add_fusion.ids, ...), custom_call_target="tpu_custom_call" | custom-call | flops 34359738368 | bytes 2097152 | tf_op jit(solution)/shard_map/products/pallas_call | solution.py:103
  26.6 4.1 %collective-permute-done.2.source = bf16[2,32,4096]{2,1,0:T(8,128)(2,1)S(1)} collective-permute-done((bf16[2,32,4096]{2,1,0:T(8,128)(2,1)S(1)}, bf16[2,32,4096]{2,1,0:T(8,128)(2,1)S(1)}, u32[]{:S(2)}, u32[]{:S(2)}) %collective-permute-start.2) | collective-permute-done | bytes 524320 | tf_op jit(solution)/shard_map/ppermute | solution.py:188
  30.8 4.7 %collective-permute-start.12 = (s16[33,16,128]{2,1,0:T(8,128)(2,1)S(1)}, s16[33,16,128]{2,1,0:T(8,128)(2,1)S(1)}, u32[]{:S(2)}, u32[]{:S(2)}) collective-permute-start(s16[33,16,128]{2,1,0:T(8,128)(2,1)S(1)} %get-tuple-element.30), channel_id=1, source_target_pairs={{0,28},{4,24},{8,20},{12,16},{16,12},{20,8},{24,4},{28,0},{1,29},{... | collective-permute-start | bytes 405512 | tf_op jit(solution)/shard_map/ppermute | solution.py:188
  35.5 0.2 collective-permute-start.13
  35.7 0.7 collective-permute-start.14
  36.5 2.1 %collective-permute-start.15 = (s16[33,16,128]{2,1,0:T(8,128)(2,1)S(1)}, s16[33,16,128]{2,1,0:T(8,128)(2,1)S(1)}, u32[]{:S(2)}, u32[]{:S(2)}) collective-permute-start(s16[33,16,128]{2,1,0:T(8,128)(2,1)S(1)} %get-tuple-element.33), channel_id=1, source_target_pairs={{0,16},{4,20},{8,24},{12,28},{16,0},{20,4},{24,8},{28,12},{1,17},{... | collective-permute-start | bytes 405512 | tf_op jit(solution)/shard_map/ppermute | solution.py:188
  38.6 2.2 %collective-permute-start.16 = (s16[33,16,128]{2,1,0:T(8,128)(2,1)S(1)}, s16[33,16,128]{2,1,0:T(8,128)(2,1)S(1)}, u32[]{:S(2)}, u32[]{:S(2)}) collective-permute-start(s16[33,16,128]{2,1,0:T(8,128)(2,1)S(1)} %get-tuple-element.34), channel_id=1, source_target_pairs={{0,12},{4,8},{8,4},{12,0},{16,28},{20,24},{24,20},{28,16},{1,13},{... | collective-permute-start | bytes 405512 | tf_op jit(solution)/shard_map/ppermute | solution.py:188
  40.8 5.8 %products.3 = (s16[33,16,128]{2,1,0:T(8,128)(2,1)S(1)}, s16[33,16,128]{2,1,0:T(8,128)(2,1)S(1)}, s16[33,16,128]{2,1,0:T(8,128)(2,1)S(1)}, s16[33,16,128]{2,1,0:T...) custom-call(s32[2]{0:T(128)S(1)} %pad_add_fusion.ids, ...), custom_call_target="tpu_custom_call" | custom-call | flops 34359738368 | bytes 2097152 | tf_op jit(solution)/shard_map/products/pallas_call | solution.py:103
  46.7 5.4 %collective-permute-start.17 = (s16[33,16,128]{2,1,0:T(8,128)(2,1)S(1)}, s16[33,16,128]{2,1,0:T(8,128)(2,1)S(1)}, u32[]{:S(2)}, u32[]{:S(2)}) collective-permute-start(s16[33,16,128]{2,1,0:T(8,128)(2,1)S(1)} %get-tuple-element.35), channel_id=1, source_target_pairs={{0,8},{4,12},{8,0},{12,4},{16,24},{20,28},{24,16},{28,20},{1,9},{5... | collective-permute-start | bytes 405512 | tf_op jit(solution)/shard_map/ppermute | solution.py:188
  52.1 1.5 %collective-permute-start.18 = (s16[33,16,128]{2,1,0:T(8,128)(2,1)S(1)}, s16[33,16,128]{2,1,0:T(8,128)(2,1)S(1)}, u32[]{:S(2)}, u32[]{:S(2)}) collective-permute-start(s16[33,16,128]{2,1,0:T(8,128)(2,1)S(1)} %get-tuple-element.36), channel_id=1, source_target_pairs={{0,4},{4,0},{8,12},{12,8},{16,20},{20,16},{24,28},{28,24},{1,5},{5... | collective-permute-start | bytes 405512 | tf_op jit(solution)/shard_map/ppermute | solution.py:188
  53.6 3.2 %collective-permute-done.14.refs_2_ = s16[33,16,128]{2,1,0:T(8,128)(2,1)S(1)} collective-permute-done((s16[33,16,128]{2,1,0:T(8,128)(2,1)S(1)}, s16[33,16,128]{2,1,0:T(8,128)(2,1)S(1)}, u32[]{:S(2)}, u32[]{:S(2)}) %collective-permute-start.14) | collective-permute-done | bytes 135200 | tf_op jit(solution)/shard_map/ppermute | solution.py:188
  56.7 3.4 %collective-permute-start.5 = (s16[33,16,128]{2,1,0:T(8,128)(2,1)S(1)}, s16[33,16,128]{2,1,0:T(8,128)(2,1)S(1)}, u32[]{:S(2)}, u32[]{:S(2)}) collective-permute-start(s16[33,16,128]{2,1,0:T(8,128)(2,1)S(1)} %get-tuple-element.22), channel_id=1, source_target_pairs={{0,28},{4,24},{8,20},{12,16},{16,12},{20,8},{24,4},{28,0},{1,29},{... | collective-permute-start | bytes 405512 | tf_op jit(solution)/shard_map/ppermute | solution.py:188
  60.2 1.9 %collective-permute-start.6 = (s16[33,16,128]{2,1,0:T(8,128)(2,1)S(1)}, s16[33,16,128]{2,1,0:T(8,128)(2,1)S(1)}, u32[]{:S(2)}, u32[]{:S(2)}) collective-permute-start(s16[33,16,128]{2,1,0:T(8,128)(2,1)S(1)} %get-tuple-element.23), channel_id=1, source_target_pairs={{0,24},{4,28},{8,16},{12,20},{16,8},{20,12},{24,0},{28,4},{1,25},{... | collective-permute-start | bytes 405512 | tf_op jit(solution)/shard_map/ppermute | solution.py:188
  62.1 2.9 %collective-permute-start.8 = (s16[33,16,128]{2,1,0:T(8,128)(2,1)S(1)}, s16[33,16,128]{2,1,0:T(8,128)(2,1)S(1)}, u32[]{:S(2)}, u32[]{:S(2)}) collective-permute-start(s16[33,16,128]{2,1,0:T(8,128)(2,1)S(1)} %get-tuple-element.25), channel_id=1, source_target_pairs={{0,16},{4,20},{8,24},{12,28},{16,0},{20,4},{24,8},{28,12},{1,17},{... | collective-permute-start | bytes 405512 | tf_op jit(solution)/shard_map/ppermute | solution.py:188
  65.0 0.6 collective-permute-start.9
  65.6 10.0 %collective-permute-start.10 = (s16[33,16,128]{2,1,0:T(8,128)(2,1)S(1)}, s16[33,16,128]{2,1,0:T(8,128)(2,1)S(1)}, u32[]{:S(2)}, u32[]{:S(2)}) collective-permute-start(s16[33,16,128]{2,1,0:T(8,128)(2,1)S(1)} %get-tuple-element.27), channel_id=1, source_target_pairs={{0,8},{4,12},{8,0},{12,4},{16,24},{20,28},{24,16},{28,20},{1,9},{5... | collective-permute-start | bytes 405512 | tf_op jit(solution)/shard_map/ppermute | solution.py:188
  75.6 0.3 collective-permute-start.11
  75.9 0.1 copy.7
  76.0 0.1 reshape.7.targets
  76.1 3.0 %tile_sums.2.refs_8_ = f32[64,8,1024]{2,1,0:T(8,128)} custom-call(s32[2]{0:T(128)S(1)} %pad_add_fusion.ids, s32[16]{0:T(128)S(1)} %reshape.7.targets, s32[8]{0:T(128)S(1)} %copy-done.2, s16[33,16,128]{2,1,0:T(8,128)(2,1)S(1)} %collective-permute-done.12.refs_0_, s16[33,16,128]{2,1,0:T(8,128)(2,1)S(1)} %collective-permute-done.13.refs_1_, ...), custom_call_target="tpu_custom_call" | custom-call | flops 2097152 | bytes 2097152 | tf_op jit(solution)/shard_map/tile_sums/pallas_call | solution.py:155
  79.1 1.7 %collective-permute-done.7.refs_2_ = s16[33,16,128]{2,1,0:T(8,128)(2,1)S(1)} collective-permute-done((s16[33,16,128]{2,1,0:T(8,128)(2,1)S(1)}, s16[33,16,128]{2,1,0:T(8,128)(2,1)S(1)}, u32[]{:S(2)}, u32[]{:S(2)}) %collective-permute-start.7) | collective-permute-done | bytes 135200 | tf_op jit(solution)/shard_map/ppermute | solution.py:188
  80.7 1.7 %collective-permute-done.8.refs_3_ = s16[33,16,128]{2,1,0:T(8,128)(2,1)S(1)} collective-permute-done((s16[33,16,128]{2,1,0:T(8,128)(2,1)S(1)}, s16[33,16,128]{2,1,0:T(8,128)(2,1)S(1)}, u32[]{:S(2)}, u32[]{:S(2)}) %collective-permute-start.8) | collective-permute-done | bytes 135200 | tf_op jit(solution)/shard_map/ppermute | solution.py:188
  82.5 1.3 %collective-permute-done.10.refs_5_ = s16[33,16,128]{2,1,0:T(8,128)(2,1)S(1)} collective-permute-done((s16[33,16,128]{2,1,0:T(8,128)(2,1)S(1)}, s16[33,16,128]{2,1,0:T(8,128)(2,1)S(1)}, u32[]{:S(2)}, u32[]{:S(2)}) %collective-permute-start.10) | collective-permute-done | bytes 135200 | tf_op jit(solution)/shard_map/ppermute | solution.py:188
  83.8 3.0 %tile_sums.3 = f32[64,8,1024]{2,1,0:T(8,128)} custom-call(s32[2]{0:T(128)S(1)} %pad_add_fusion.ids, s32[16]{0:T(128)S(1)} %reshape.7.targets, s32[8]{0:T(128)S(1)} %copy-done.2, s16[33,16,128]{2,1,0:T(8,128)(2,1)S(1)} %collective-permute-done.5.refs_0_, s16[33,16,128]{2,1,0:T(8,128)(2,1)S(1)} %collective-permute-done.6.refs_1_, ...), custom_call_target="tpu_custom_call", output_to_operand_aliasing={{}: (11, {})} | custom-call | flops 2097152 | bytes 2097152 | tf_op jit(solution)/shard_map/tile_sums/pallas_call | solution.py:155
  (27 shorter events, 0.4 us)
Async XLA Ops:
  0.0 18.8 %collective-permute-start.1 = (bf16[2,64,4096]{2,1,0:T(8,128)(2,1)}, bf16[2,64,4096]{2,1,0:T(8,128)(2,1)S(1)}, u32[]{:S(2)}, u32[]{:S(2)}) collective-permute-start(bf16[2,64,4096]{2,1,0:T(8,128)(2,1)} %bitcast.3), channel_id=1, source_target_pairs={{0,1},{1,0},{2,3},{3,2},{4,5},{5,4},{6,7},{7,6},{8,9},{9,8},{10,11... | collective-permute-start | bytes 3145736 | tf_op jit(solution)/shard_map/ppermute | solution.py:188
  0.5 1.2 %copy-start = (bf16[128,1,4096]{2,0,1:T(8,128)(2,1)S(1)}, bf16[128,1,4096]{2,0,1:T(8,128)(2,1)}, u32[]{:S(2)}) copy-start(bf16[128,1,4096]{2,0,1:T(8,128)(2,1)} %param.4) | copy-start | bytes 3145732
  1.7 15.2 %collective-permute-start = (bf16[2,32,4096]{2,1,0:T(8,128)(2,1)S(1)}, bf16[2,32,4096]{2,1,0:T(8,128)(2,1)S(1)}, u32[]{:S(2)}, u32[]{:S(2)}) collective-permute-start(bf16[2,32,4096]{2,1,0:T(8,128)(2,1)S(1)} %picked_rows.4.refs_0_), channel_id=1, source_target_pairs={{0,2},{1,3},{2,0},{3,1},{4,6},{5,7},{6,4},{7,5},{8,10},{9,11},{10,... | collective-permute-start | bytes 1572872 | tf_op jit(solution)/shard_map/ppermute | solution.py:188
  4.3 12.6 %copy-start.1 = (bf16[128,1,4096]{2,0,1:T(8,128)(2,1)S(1)}, bf16[128,1,4096]{2,0,1:T(8,128)(2,1)}, u32[]{:S(2)}) copy-start(bf16[128,1,4096]{2,0,1:T(8,128)(2,1)} %param.4) | copy-start | bytes 3145732
  16.9 13.8 %collective-permute-start.2 = (bf16[2,32,4096]{2,1,0:T(8,128)(2,1)S(1)}, bf16[2,32,4096]{2,1,0:T(8,128)(2,1)S(1)}, u32[]{:S(2)}, u32[]{:S(2)}) collective-permute-start(bf16[2,32,4096]{2,1,0:T(8,128)(2,1)S(1)} %picked_rows.5.refs_0_), channel_id=1, source_target_pairs={{0,2},{1,3},{2,0},{3,1},{4,6},{5,7},{6,4},{7,5},{8,10},{9,11},{10,... | collective-permute-start | bytes 1572872 | tf_op jit(solution)/shard_map/ppermute | solution.py:188
  18.8 2.0 %collective-permute-start.3 = (bf16[2,32,4096]{2,1,0:T(8,128)(2,1)S(1)}, bf16[2,32,4096]{2,1,0:T(8,128)(2,1)S(1)}, u32[]{:S(2)}, u32[]{:S(2)}) collective-permute-start(bf16[2,32,4096]{2,1,0:T(8,128)(2,1)S(1)} %picked_rows.6.refs_2_), channel_id=1, source_target_pairs={{0,1},{1,0},{2,3},{3,2},{4,5},{5,4},{6,7},{7,6},{8,9},{9,8},{10,11... | collective-permute-start | bytes 1572872 | tf_op jit(solution)/shard_map/ppermute | solution.py:188
  30.8 7.8 %collective-permute-start.4 = (bf16[2,32,4096]{2,1,0:T(8,128)(2,1)S(1)}, bf16[2,32,4096]{2,1,0:T(8,128)(2,1)S(1)}, u32[]{:S(2)}, u32[]{:S(2)}) collective-permute-start(bf16[2,32,4096]{2,1,0:T(8,128)(2,1)S(1)} %picked_rows.7.refs_2_), channel_id=1, source_target_pairs={{0,1},{1,0},{2,3},{3,2},{4,5},{5,4},{6,7},{7,6},{8,9},{9,8},{10,11... | collective-permute-start | bytes 1572872 | tf_op jit(solution)/shard_map/ppermute | solution.py:188
  30.8 15.8 %collective-permute-start.12 = (s16[33,16,128]{2,1,0:T(8,128)(2,1)S(1)}, s16[33,16,128]{2,1,0:T(8,128)(2,1)S(1)}, u32[]{:S(2)}, u32[]{:S(2)}) collective-permute-start(s16[33,16,128]{2,1,0:T(8,128)(2,1)S(1)} %get-tuple-element.30), channel_id=1, source_target_pairs={{0,28},{4,24},{8,20},{12,16},{16,12},{20,8},{24,4},{28,0},{1,29},{... | collective-permute-start | bytes 405512 | tf_op jit(solution)/shard_map/ppermute | solution.py:188
  35.5 16.5 %collective-permute-start.13 = (s16[33,16,128]{2,1,0:T(8,128)(2,1)S(1)}, s16[33,16,128]{2,1,0:T(8,128)(2,1)S(1)}, u32[]{:S(2)}, u32[]{:S(2)}) collective-permute-start(s16[33,16,128]{2,1,0:T(8,128)(2,1)S(1)} %get-tuple-element.31), channel_id=1, source_target_pairs={{0,24},{4,28},{8,16},{12,20},{16,8},{20,12},{24,0},{28,4},{1,25},{... | collective-permute-start | bytes 405512 | tf_op jit(solution)/shard_map/ppermute | solution.py:188
  35.7 21.0 %collective-permute-start.14 = (s16[33,16,128]{2,1,0:T(8,128)(2,1)S(1)}, s16[33,16,128]{2,1,0:T(8,128)(2,1)S(1)}, u32[]{:S(2)}, u32[]{:S(2)}) collective-permute-start(s16[33,16,128]{2,1,0:T(8,128)(2,1)S(1)} %get-tuple-element.32), channel_id=1, source_target_pairs={{0,20},{4,16},{8,28},{12,24},{16,4},{20,0},{24,12},{28,8},{1,21},{... | collective-permute-start | bytes 405512 | tf_op jit(solution)/shard_map/ppermute | solution.py:188
  36.5 23.7 %collective-permute-start.15 = (s16[33,16,128]{2,1,0:T(8,128)(2,1)S(1)}, s16[33,16,128]{2,1,0:T(8,128)(2,1)S(1)}, u32[]{:S(2)}, u32[]{:S(2)}) collective-permute-start(s16[33,16,128]{2,1,0:T(8,128)(2,1)S(1)} %get-tuple-element.33), channel_id=1, source_target_pairs={{0,16},{4,20},{8,24},{12,28},{16,0},{20,4},{24,8},{28,12},{1,17},{... | collective-permute-start | bytes 405512 | tf_op jit(solution)/shard_map/ppermute | solution.py:188
  38.6 23.5 %collective-permute-start.16 = (s16[33,16,128]{2,1,0:T(8,128)(2,1)S(1)}, s16[33,16,128]{2,1,0:T(8,128)(2,1)S(1)}, u32[]{:S(2)}, u32[]{:S(2)}) collective-permute-start(s16[33,16,128]{2,1,0:T(8,128)(2,1)S(1)} %get-tuple-element.34), channel_id=1, source_target_pairs={{0,12},{4,8},{8,4},{12,0},{16,28},{20,24},{24,20},{28,16},{1,13},{... | collective-permute-start | bytes 405512 | tf_op jit(solution)/shard_map/ppermute | solution.py:188
  40.8 35.1 %copy-start.3 = (s32[8,2]{0,1:T(2,128)S(1)}, s32[8,2]{0,1:T(2,128)}, u32[]{:S(2)}) copy-start(s32[8,2]{0,1:T(2,128)} %param.6) | copy-start | bytes 196
  40.8 35.3 %copy-start.2 = (s32[8]{0:T(128)S(1)}, s32[8]{0:T(128)}, u32[]{:S(2)}) copy-start(s32[8]{0:T(128)} %counts.3) | copy-start | bytes 100
  46.7 15.4 %collective-permute-start.17 = (s16[33,16,128]{2,1,0:T(8,128)(2,1)S(1)}, s16[33,16,128]{2,1,0:T(8,128)(2,1)S(1)}, u32[]{:S(2)}, u32[]{:S(2)}) collective-permute-start(s16[33,16,128]{2,1,0:T(8,128)(2,1)S(1)} %get-tuple-element.35), channel_id=1, source_target_pairs={{0,8},{4,12},{8,0},{12,4},{16,24},{20,28},{24,16},{28,20},{1,9},{5... | collective-permute-start | bytes 405512 | tf_op jit(solution)/shard_map/ppermute | solution.py:188
  52.1 12.9 %collective-permute-start.18 = (s16[33,16,128]{2,1,0:T(8,128)(2,1)S(1)}, s16[33,16,128]{2,1,0:T(8,128)(2,1)S(1)}, u32[]{:S(2)}, u32[]{:S(2)}) collective-permute-start(s16[33,16,128]{2,1,0:T(8,128)(2,1)S(1)} %get-tuple-element.36), channel_id=1, source_target_pairs={{0,4},{4,0},{8,12},{12,8},{16,20},{20,16},{24,28},{28,24},{1,5},{5... | collective-permute-start | bytes 405512 | tf_op jit(solution)/shard_map/ppermute | solution.py:188
  56.7 8.9 %collective-permute-start.5 = (s16[33,16,128]{2,1,0:T(8,128)(2,1)S(1)}, s16[33,16,128]{2,1,0:T(8,128)(2,1)S(1)}, u32[]{:S(2)}, u32[]{:S(2)}) collective-permute-start(s16[33,16,128]{2,1,0:T(8,128)(2,1)S(1)} %get-tuple-element.22), channel_id=1, source_target_pairs={{0,28},{4,24},{8,20},{12,16},{16,12},{20,8},{24,4},{28,0},{1,29},{... | collective-permute-start | bytes 405512 | tf_op jit(solution)/shard_map/ppermute | solution.py:188
  60.2 15.4 %collective-permute-start.6 = (s16[33,16,128]{2,1,0:T(8,128)(2,1)S(1)}, s16[33,16,128]{2,1,0:T(8,128)(2,1)S(1)}, u32[]{:S(2)}, u32[]{:S(2)}) collective-permute-start(s16[33,16,128]{2,1,0:T(8,128)(2,1)S(1)} %get-tuple-element.23), channel_id=1, source_target_pairs={{0,24},{4,28},{8,16},{12,20},{16,8},{20,12},{24,0},{28,4},{1,25},{... | collective-permute-start | bytes 405512 | tf_op jit(solution)/shard_map/ppermute | solution.py:188
  62.1 18.6 %collective-permute-start.7 = (s16[33,16,128]{2,1,0:T(8,128)(2,1)S(1)}, s16[33,16,128]{2,1,0:T(8,128)(2,1)S(1)}, u32[]{:S(2)}, u32[]{:S(2)}) collective-permute-start(s16[33,16,128]{2,1,0:T(8,128)(2,1)S(1)} %get-tuple-element.24), channel_id=1, source_target_pairs={{0,20},{4,16},{8,28},{12,24},{16,4},{20,0},{24,12},{28,8},{1,21},{... | collective-permute-start | bytes 405512 | tf_op jit(solution)/shard_map/ppermute | solution.py:188
  62.1 20.3 %collective-permute-start.8 = (s16[33,16,128]{2,1,0:T(8,128)(2,1)S(1)}, s16[33,16,128]{2,1,0:T(8,128)(2,1)S(1)}, u32[]{:S(2)}, u32[]{:S(2)}) collective-permute-start(s16[33,16,128]{2,1,0:T(8,128)(2,1)S(1)} %get-tuple-element.25), channel_id=1, source_target_pairs={{0,16},{4,20},{8,24},{12,28},{16,0},{20,4},{24,8},{28,12},{1,17},{... | collective-permute-start | bytes 405512 | tf_op jit(solution)/shard_map/ppermute | solution.py:188
  65.0 17.5 %collective-permute-start.9 = (s16[33,16,128]{2,1,0:T(8,128)(2,1)S(1)}, s16[33,16,128]{2,1,0:T(8,128)(2,1)S(1)}, u32[]{:S(2)}, u32[]{:S(2)}) collective-permute-start(s16[33,16,128]{2,1,0:T(8,128)(2,1)S(1)} %get-tuple-element.26), channel_id=1, source_target_pairs={{0,12},{4,8},{8,4},{12,0},{16,28},{20,24},{24,20},{28,16},{1,13},{... | collective-permute-start | bytes 405512 | tf_op jit(solution)/shard_map/ppermute | solution.py:188
  65.6 18.2 %collective-permute-start.10 = (s16[33,16,128]{2,1,0:T(8,128)(2,1)S(1)}, s16[33,16,128]{2,1,0:T(8,128)(2,1)S(1)}, u32[]{:S(2)}, u32[]{:S(2)}) collective-permute-start(s16[33,16,128]{2,1,0:T(8,128)(2,1)S(1)} %get-tuple-element.27), channel_id=1, source_target_pairs={{0,8},{4,12},{8,0},{12,4},{16,24},{20,28},{24,16},{28,20},{1,9},{5... | collective-permute-start | bytes 405512 | tf_op jit(solution)/shard_map/ppermute | solution.py:188
  75.6 8.2 %collective-permute-start.11 = (s16[33,16,128]{2,1,0:T(8,128)(2,1)S(1)}, s16[33,16,128]{2,1,0:T(8,128)(2,1)S(1)}, u32[]{:S(2)}, u32[]{:S(2)}) collective-permute-start(s16[33,16,128]{2,1,0:T(8,128)(2,1)S(1)} %get-tuple-element.28), channel_id=1, source_target_pairs={{0,4},{4,0},{8,12},{12,8},{16,20},{20,16},{24,28},{28,24},{1,5},{5... | collective-permute-start | bytes 405512 | tf_op jit(solution)/shard_map/ppermute | solution.py:188

commit v2 on v1

v2 whole, which is shorter than its diff:
```python
import functools

import jax
import jax.numpy as jnp
from jax import lax
from jax.experimental import pallas as pl
from jax.experimental.pallas import tpu as pltpu
from jax.sharding import PartitionSpec as P

MIB = 1 << 20
TOP = 32766.0
MANT = 8192.0
WORK = 16


def scale_code(peak):
    exponent = jnp.clip(jnp.floor(jnp.log2(jnp.maximum(peak, 1e-37))), -125.0, 125.0)
    mantissa = jnp.minimum(jnp.ceil(peak * jnp.exp2(-exponent) * MANT) + 1.0, 32000.0)
    return exponent, jnp.maximum(mantissa, 1.0)


def pick_kernel(start, source, *refs):
    out, done = refs[-2:]
    copy = pltpu.make_async_copy(source.at[:, pl.ds(start, out.shape[1]), :], out, done)
    copy.start()
    copy.wait()


def picked(source, start, rows, after):
    share, _, depth = source.shape
    return pl.pallas_call(
        functools.partial(pick_kernel, start),
        out_shape=jax.ShapeDtypeStruct((share, rows, depth), source.dtype),
        in_specs=[pl.BlockSpec(memory_space=pl.ANY)] * (1 + len(after)),
        out_specs=pl.BlockSpec(memory_space=pltpu.VMEM),
        scratch_shapes=[pltpu.SemaphoreType.DMA],
        compiler_params=pltpu.CompilerParams(vmem_limit_bytes=8 * MIB),
        name="picked_rows",
    )(source, *after)


def multiply_and_code(left, total, multiply, slots, cols, parts, put):
    height, lanes = sum(parts), cols // 128
    blocks = left.shape[0] // height

    lane = lax.broadcasted_iota(jnp.int32, (16, 128), 1)

    def one_slot(slot, codes):
        multiply(slot)
        codes = list(codes)
        for b in range(blocks):
            first = b * height
            for c, rows in enumerate(parts):
                for g in range(rows // 16):
                    value = total[first : first + 16, :]
                    first += 16
                    peak = jnp.max(jnp.abs(value), axis=1, keepdims=True)
                    exponent, mantissa = scale_code(peak)
                    value = value * jnp.exp2(-exponent) * (TOP * MANT / mantissa)
                    value = jnp.round(value).astype(jnp.int32).astype(jnp.int16)
                    at = (slot * (rows // 16) + g) * lanes
                    for t in range(lanes):
                        put(c, b, at + t, value[:, t * 128 : t * 128 + 128])
                    spot = (slot * (rows // 16) + g) * 2
                    code = codes[b * len(parts) + c]
                    code = jnp.where(lane == spot, exponent.astype(jnp.int32), code)
                    codes[b * len(parts) + c] = jnp.where(lane == spot + 1, mantissa.astype(jnp.int32), code)
        return tuple(codes)

    empty = tuple(jnp.zeros((16, 128), jnp.int32) for _ in range(blocks * len(parts)))
    codes = lax.fori_loop(0, slots, one_slot, empty)
    for b in range(blocks):
        for c, rows in enumerate(parts):
            put(c, b, slots * (rows // 16) * lanes, codes[b * len(parts) + c].astype(jnp.int16))


def stage_kernel(source, kept, done):
    copy = pltpu.make_async_copy(source, kept, done)
    copy.start()
    copy.wait()


def staged(integrals):
    return pl.pallas_call(
        stage_kernel,
        out_shape=pltpu.VMEM(integrals.shape, integrals.dtype),
        in_specs=[pl.BlockSpec(memory_space=pltpu.HBM)],
        out_specs=pl.BlockSpec(memory_space=pltpu.VMEM),
        scratch_shapes=[pltpu.SemaphoreType.DMA],
        compiler_params=pltpu.CompilerParams(vmem_limit_bytes=40 * MIB),
        name="staged_integrals",
    )(integrals)


def multiplied(left, kept, total):
    def multiply(slot):
        for n in range(0, kept.shape[3], 256):
            wide = slice(n, n + 256)
            total[:, wide] = jnp.dot(left[...], kept[0, slot, :, wide], preferred_element_type=jnp.float32)

    return multiply


def near_kernel(slots, share, waits, *refs):
    own, beside, kept, out, left, total = refs[waits:]
    rows = own.shape[1]
    for k, piece in enumerate((own, beside)):
        for sub in range(share):
            left[(k * share + sub) * rows : (k * share + sub + 1) * rows, :] = piece[sub]

    def put(c, b, tile, value):
        out[b, tile] = value

    multiply_and_code(left, total, multiplied(left, kept, total), slots, kept.shape[3], (rows,), put)


def far_kernel(slots, wide, count, share, rows, waits, early_count, ids, *refs):
    refs = refs[waits:]
    pieces, early, kept = refs[:count], refs[count : count + early_count], refs[count + early_count]
    outs = refs[count + early_count + 1 : -3]
    left, total, ready = refs[-3:]
    cols = kept.shape[3]
    me, mine = ids[0], ids[1]
    tiles = ready.shape[1]
    blocks = [(piece, at) for piece in pieces for at in range(piece.shape[0])]
    for b, (piece, at) in enumerate(blocks):
        left[b * rows : (b + 1) * rows, :] = piece[at]

    def place(k, sub):
        return ((mine ^ k) * share + sub) ^ me

    def put(c, b, tile, value):
        ready[place(2 * early_count + b // share, b % share), tile] = value

    for given in early:
        for b in range(given.shape[0]):
            ready[place(b // share, b % share)] = given[b]
    multiply_and_code(left, total, multiplied(left, kept, total), slots, cols, (rows,), put)
    for s in range(wide):
        outs[s][...] = ready[s]


def tile_count(slots, rows, cols):
    return slots * (rows // 16) * (cols // 128) + 1


def near_products(own, beside, integrals, after):
    _, slots, depth, cols = integrals.shape
    share, rows, _ = own.shape
    vmem = pl.BlockSpec(memory_space=pltpu.VMEM)
    return pl.pallas_call(
        functools.partial(near_kernel, slots, share, len(after)),
        out_shape=jax.ShapeDtypeStruct((2 * share, tile_count(slots, rows, cols), 16, 128), jnp.int16),
        in_specs=[pl.BlockSpec(memory_space=pl.ANY)] * len(after) + [vmem] * 3,
        out_specs=vmem,
        scratch_shapes=[
            pltpu.VMEM((2 * share * rows, depth), integrals.dtype),
            pltpu.VMEM((2 * share * rows, cols), jnp.float32),
        ],
        compiler_params=pltpu.CompilerParams(vmem_limit_bytes=16 * MIB),
        cost_estimate=pl.CostEstimate(
            flops=WORK * slots * 2 * share * rows * depth * cols,
            bytes_accessed=4 * share * rows * depth,
            transcendentals=0,
        ),
        name="near_products",
    )(*after, own, beside, integrals)


def far_products(ids, pieces, early, integrals, wide, share, after):
    _, slots, depth, cols = integrals.shape
    count, rows = len(pieces), pieces[0].shape[1]
    blocks = sum(piece.shape[0] for piece in pieces)
    tiles = tile_count(slots, rows, cols)
    vmem = pl.BlockSpec(memory_space=pltpu.VMEM)
    return pl.pallas_call(
        functools.partial(far_kernel, slots, wide, count, share, rows, len(after), len(early)),
        out_shape=[jax.ShapeDtypeStruct((tiles, 16, 128), jnp.int16)] * wide,
        in_specs=[pl.BlockSpec(memory_space=pltpu.SMEM)]
        + [pl.BlockSpec(memory_space=pl.ANY)] * len(after)
        + [vmem] * (count + len(early) + 1),
        out_specs=[vmem] * wide,
        scratch_shapes=[
            pltpu.VMEM((blocks * rows, depth), integrals.dtype),
            pltpu.VMEM((blocks * rows, cols), jnp.float32),
            pltpu.VMEM((wide, tiles, 16, 128), jnp.int16),
        ],
        compiler_params=pltpu.CompilerParams(vmem_limit_bytes=16 * MIB),
        cost_estimate=pl.CostEstimate(
            flops=WORK * slots * blocks * rows * depth * cols,
            bytes_accessed=2 * blocks * rows * depth,
            transcendentals=0,
        ),
        name="far_products",
    )(ids, *after, *pieces, *early, integrals)


def sum_kernel(slots, plan, start, rows, cols, ids, targets, counts, *refs):
    out, total, turned, done = refs[-4:]
    me = ids[0]
    groups, lanes = rows // 16, cols // 128
    tiles = slots * groups * lanes + 1
    total[...] = jnp.zeros_like(total)
    lane = lax.broadcasted_iota(jnp.int32, (16, 128), 1)
    for index, bits, at in plan:
        panel = me ^ bits
        codes = refs[index][at + tiles - 1].astype(jnp.int32)
        for j in range(slots):

            @pl.when(j < counts[panel])
            def add():
                tile = targets[panel * slots + j]
                for g in range(groups):
                    spot = (j * groups + g) * 2
                    exponent = jnp.sum(jnp.where(lane == spot, codes, 0).astype(jnp.float32), axis=1, keepdims=True)
                    mantissa = jnp.sum(jnp.where(lane == spot + 1, codes, 0).astype(jnp.float32), axis=1, keepdims=True)
                    scale = jnp.exp2(exponent) * (mantissa * (1.0 / (TOP * MANT)))
                    for t in range(lanes):
                        value = refs[index][at + (j * groups + g) * lanes + t].astype(jnp.int32).astype(jnp.float32)
                        total[tile, g * 16 : g * 16 + 16, t * 128 : t * 128 + 128] += value * scale
    copies = []
    for g in range(rows // 8):
        part = slice(g * 8, g * 8 + 8)
        for t in range(lanes):
            span = slice(t * 128, t * 128 + 128)
            turned[part, :, span] = jnp.swapaxes(total[:, part, span], 0, 1)
        copies.append(pltpu.make_async_copy(turned.at[part], out.at[pl.ds(start + g * 8, 8)], done.at[g]))
        copies[-1].start()
    for copy in copies:
        copy.wait()


def summed(ids, targets, counts, given, plan, held, start, rows, cols, height):
    pairs, slots = targets.shape
    extra = [] if held is None else [held]
    smem, vmem = pl.BlockSpec(memory_space=pltpu.SMEM), pl.BlockSpec(memory_space=pltpu.VMEM)
    return pl.pallas_call(
        functools.partial(sum_kernel, slots, plan, start, rows, cols),
        out_shape=jax.ShapeDtypeStruct((height, pairs, cols), jnp.float32),
        in_specs=[smem] * 3 + [vmem] * len(given) + [pl.BlockSpec(memory_space=pl.ANY)] * len(extra),
        out_specs=pl.BlockSpec(memory_space=pl.ANY),
        scratch_shapes=[
            pltpu.VMEM((pairs, rows, cols), jnp.float32),
            pltpu.VMEM((rows, pairs, cols), jnp.float32),
            pltpu.SemaphoreType.DMA((rows // 8,)),
        ],
        input_output_aliases={3 + len(given): 0} if extra else {},
        compiler_params=pltpu.CompilerParams(vmem_limit_bytes=32 * MIB),
        cost_estimate=pl.CostEstimate(
            flops=4 * pairs * slots * rows * cols,
            bytes_accessed=2 * pairs * slots * rows * cols + 4 * pairs * rows * cols,
            transcendentals=0,
        ),
        name="tile_sums",
    )(ids, targets.reshape(-1), counts, *given, *extra)


def on_device(amplitudes, integrals, targets, counts):
    wide, narrow = lax.axis_size("wide"), lax.axis_size("narrow")
    me, mine = lax.axis_index("wide"), lax.axis_index("narrow")
    ids = jnp.stack([me, mine]).astype(jnp.int32)
    depth, cols = integrals.shape[2], integrals.shape[3]
    share = wide // narrow
    height = amplitudes.shape[0] // share
    own = amplitudes.reshape(share, height, depth)
    parts = (height // 2, height - height // 2)

    def across(array, axis, size, bits):
        return lax.ppermute(array, axis, [(i, i ^ bits) for i in range(size)])

    starts = [sum(parts[:i]) for i in range(len(parts))]
    beside = across(own, "narrow", narrow, 1)
    kept = staged(integrals)
    both = jnp.concatenate([own[:, parts[0] :], beside[:, parts[0] :]])
    received, after, waits = [], [], []
    for start, rows in zip(starts, parts):
        chunk = picked(both, start - parts[0], rows, after) if start else picked(own, start, rows, after)
        far = [across(chunk, "narrow", narrow, k) for k in range(2, narrow, 2)]
        after = far[-1:]
        early = [near_products(own[:, start : start + rows], beside[:, start : start + rows], kept, waits)]
        if not start:
            odd = [across(picked(c, 0, rows, [kept, *early]), "narrow", narrow, 1) for c in far]
            pieces = [piece for pair in zip(far, odd) for piece in pair]
        else:
            pieces = far
        sent = far_products(ids, pieces, early, kept, wide, share, waits)
        waits = [sent[0]]
        crossing, others = [*range(wide // 2, wide)], [*range(2, wide // 2)]
        order = [1, *others[:1], *crossing, *others[1:]] if rows == height - start else [*crossing, 1, *others]
        given = [across(sent[s], "wide", wide, s) for s in order] + [sent[0]]
        received.append((given, tuple((i, s, 0) for i, s in enumerate([*order, 0]))))
    held = None
    for (given, plan), start, rows in zip(received, starts, parts):
        held = summed(ids, targets, counts, given, plan, held, start, rows, cols, height)
    return held


def solution(mesh):
    in_specs = (P("narrow", "wide", None), P("wide", None, None, "narrow"), P(), P())
    out_specs = P("wide", None, "narrow")
    return jax.shard_map(
        on_device, mesh=mesh, in_specs=in_specs, out_specs=out_specs, check_vma=False
    )
```

time: 86.8 us -> 80.2 us (0.924)
  the two profiles are of different devices: /device:TPU:0 before, /device:TPU:10 now
where the time goes in v2:
time: 80.2 us; the launch traced here: 80.1 us
  starting transfers between devices  27.3 us (34%)
  waiting for transfers between devices  25.8 us (32%)
  Pallas kernels  25 us (31%)
  local copies, waits for them, and re-layouts  1.67 us (2%)
    ppermute x18, starting transfers between devices, across(): return lax.ppermute(array, axis, [(i, i ^ bits) for i in range(size)])  27.3 us
    ppermute x18, waiting for transfers between devices, across(): return lax.ppermute(array, axis, [(i, i ^ bits) for i in range(size)])  25.8 us
    pallas_call x2, Pallas kernels, far_products(): pl.pallas_call(functools.partial(far_kernel, slots, wide, count, share, r...  7.24 us
    pallas_call x2, Pallas kernels, near_products(): pl.pallas_call(functools.partial(near_kernel, slots, share, len(after)),...  5.94 us
    pallas_call x1, Pallas kernels, staged(): pl.pallas_call(stage_kernel, out_shape=pltpu.VMEM(integrals.shape, integr...  5.87 us
    pallas_call x2, Pallas kernels, summed(): pl.pallas_call(functools.partial(sum_kernel, slots, plan, start, rows, co...  5.77 us
  transfers between devices with their start and end apart: 18, of which 6 were waited for; matrix products, arithmetic and copies ran while one was open for 1% of the time, Pallas kernels for 28%

profile of v2, /device:TPU:10, one launch (start us, length us, event | category | flops | bytes accessed | tf_op | source)
XLA Modules:
  0.0 80.1 jit_solution(17407783926227997644)
XLA Ops:
  0.0 1.2 %copy-done = bf16[128,1,4096]{2,0,1:T(8,128)(2,1)S(1)} copy-done((bf16[128,1,4096]{2,0,1:T(8,128)(2,1)S(1)}, bf16[128,1,4096]{2,0,1:T(8,128)(2,1)}, u32[]{:S(2)}) %copy-start) | copy-done | bytes 1048600
  1.3 0.6 collective-permute-start
  1.9 5.9 %staged_integrals.1.refs_2_.refs_0_.refs_3_ = bf16[1,2,4096,1024]{3,2,1,0:T(8,128)(2,1)S(1)} custom-call(bf16[1,2,4096,1024]{3,2,1,0:T(8,128)(2,1)} %source.1), custom_call_target="tpu_custom_call" | custom-call | tf_op jit(solution)/shard_map/staged_integrals/pallas_call | solution.py:84
  7.8 0.1 copy-done.1
  8.1 3.0 %near_products.2.refs_1_.refs_2_ = s16[4,33,16,128]{3,2,1,0:T(8,128)(2,1)S(1)} custom-call(bf16[2,32,4096]{2,1,0:T(8,128)(2,1)S(1)} %get-tuple-element.38.refs_0_, bf16[2,32,4096]{2,1,0:T(8,128)(2,1)S(1)} %get-tuple-element.40.refs_1_, bf16[1,2,4096,1024]{3,2,1,0:T(8,128)(2,1)S(1)} %staged_integrals.1.refs_2_.refs_0_.refs_3_), custom_call_target="tpu_custom_call" | custom-call | flops 17179869184 | bytes 1048576 | tf_op jit(solution)/shard_map/near_products/pallas_call | solution.py:151
  11.0 4.7 %collective-permute-done.source.refs_0_ = bf16[2,32,4096]{2,1,0:T(8,128)(2,1)S(1)} collective-permute-done((bf16[2,32,4096]{2,1,0:T(8,128)(2,1)S(1)}, bf16[2,32,4096]{2,1,0:T(8,128)(2,1)S(1)}, u32[]{:S(2)}, u32[]{:S(2)}) %collective-permute-start) | collective-permute-done | bytes 524320 | tf_op jit(solution)/shard_map/ppermute | solution.py:269
  15.9 0.1 pad_maximum_fusion.source
  16.1 0.6 collective-permute-start.3
  16.7 1.0 %collective-permute-done.2.refs_1_ = bf16[2,32,4096]{2,1,0:T(8,128)(2,1)S(1)} collective-permute-done((bf16[2,32,4096]{2,1,0:T(8,128)(2,1)S(1)}, bf16[2,32,4096]{2,1,0:T(8,128)(2,1)S(1)}, u32[]{:S(2)}, u32[]{:S(2)}) %collective-permute-start.2) | collective-permute-done | bytes 524320 | tf_op jit(solution)/shard_map/ppermute | solution.py:269
  17.7 3.6 %far_products.2 = (s16[33,16,128]{2,1,0:T(8,128)(2,1)S(1)}, s16[33,16,128]{2,1,0:T(8,128)(2,1)S(1)}, s16[33,16,128]{2,1,0:T(8,128)(2,1)S(1)}, s16[33,16,128]{2,1...) custom-call(s32[2]{0:T(128)S(1)} %pad_add_fusion.ids, ...), custom_call_target="tpu_custom_call" | custom-call | flops 17179869184 | bytes 1048576 | tf_op jit(solution)/shard_map/far_products/pallas_call | solution.py:176
  21.4 2.6 %collective-permute-start.11 = (s16[33,16,128]{2,1,0:T(8,128)(2,1)S(1)}, s16[33,16,128]{2,1,0:T(8,128)(2,1)S(1)}, u32[]{:S(2)}, u32[]{:S(2)}) collective-permute-start(s16[33,16,128]{2,1,0:T(8,128)(2,1)S(1)} %get-tuple-element.30), channel_id=1, source_target_pairs={{0,16},{4,20},{8,24},{12,28},{16,0},{20,4},{24,8},{28,12},{1,17},{... | collective-permute-start | bytes 405512 | tf_op jit(solution)/shard_map/ppermute | solution.py:269
  24.0 1.3 %collective-permute-start.12 = (s16[33,16,128]{2,1,0:T(8,128)(2,1)S(1)}, s16[33,16,128]{2,1,0:T(8,128)(2,1)S(1)}, u32[]{:S(2)}, u32[]{:S(2)}) collective-permute-start(s16[33,16,128]{2,1,0:T(8,128)(2,1)S(1)} %get-tuple-element.31), channel_id=1, source_target_pairs={{0,20},{4,16},{8,28},{12,24},{16,4},{20,0},{24,12},{28,8},{1,21},{... | collective-permute-start | bytes 405512 | tf_op jit(solution)/shard_map/ppermute | solution.py:269
  25.3 1.6 %collective-permute-start.13 = (s16[33,16,128]{2,1,0:T(8,128)(2,1)S(1)}, s16[33,16,128]{2,1,0:T(8,128)(2,1)S(1)}, u32[]{:S(2)}, u32[]{:S(2)}) collective-permute-start(s16[33,16,128]{2,1,0:T(8,128)(2,1)S(1)} %get-tuple-element.32), channel_id=1, source_target_pairs={{0,24},{4,28},{8,16},{12,20},{16,8},{20,12},{24,0},{28,4},{1,25},{... | collective-permute-start | bytes 405512 | tf_op jit(solution)/shard_map/ppermute | solution.py:269
  26.9 0.4 collective-permute-start.14
  27.3 3.0 %near_products.3.refs_2_ = s16[4,33,16,128]{3,2,1,0:T(8,128)(2,1)S(1)} custom-call(s16[33,16,128]{2,1,0:T(8,128)(2,1)S(1)} %get-tuple-element.21.refs_0_.refs_7_, bf16[2,32,4096]{2,1,0:T(8,128)(2,1)S(1)} %get-tuple-element.37.refs_1_, bf16[2,32,4096]{2,1,0:T(8,128)(2,1)S(1)} %get-tuple-element.39.refs_2_, ...), custom_call_target="tpu_custom_call" | custom-call | flops 17179869184 | bytes 1048576 | tf_op jit(solution)/shard_map/near_products/pallas_call | solution.py:151
  30.2 11.5 %collective-permute-done.3.refs_1_ = bf16[4,32,4096]{2,1,0:T(8,128)(2,1)S(1)} collective-permute-done((bf16[4,32,4096]{2,1,0:T(8,128)(2,1)S(1)}, bf16[4,32,4096]{2,1,0:T(8,128)(2,1)S(1)}, u32[]{:S(2)}, u32[]{:S(2)}) %collective-permute-start.3) | collective-permute-done | bytes 1048608 | tf_op jit(solution)/shard_map/ppermute | solution.py:269
  41.7 1.5 %collective-permute-start.15 = (s16[33,16,128]{2,1,0:T(8,128)(2,1)S(1)}, s16[33,16,128]{2,1,0:T(8,128)(2,1)S(1)}, u32[]{:S(2)}, u32[]{:S(2)}) collective-permute-start(s16[33,16,128]{2,1,0:T(8,128)(2,1)S(1)} %get-tuple-element.34), channel_id=1, source_target_pairs={{0,4},{4,0},{8,12},{12,8},{16,20},{20,16},{24,28},{28,24},{1,5},{5... | collective-permute-start | bytes 405512 | tf_op jit(solution)/shard_map/ppermute | solution.py:269
  43.2 3.6 %far_products.3 = (s16[33,16,128]{2,1,0:T(8,128)(2,1)S(1)}, s16[33,16,128]{2,1,0:T(8,128)(2,1)S(1)}, s16[33,16,128]{2,1,0:T(8,128)(2,1)S(1)}, s16[33,16,128]{2,1...) custom-call(s32[2]{0:T(128)S(1)} %pad_add_fusion.ids, ...), custom_call_target="tpu_custom_call" | custom-call | flops 17179869184 | bytes 1048576 | tf_op jit(solution)/shard_map/far_products/pallas_call | solution.py:176
  46.9 0.5 collective-permute-start.16
  47.4 1.5 %collective-permute-start.17 = (s16[33,16,128]{2,1,0:T(8,128)(2,1)S(1)}, s16[33,16,128]{2,1,0:T(8,128)(2,1)S(1)}, u32[]{:S(2)}, u32[]{:S(2)}) collective-permute-start(s16[33,16,128]{2,1,0:T(8,128)(2,1)S(1)} %get-tuple-element.36), channel_id=1, source_target_pairs={{0,12},{4,8},{8,4},{12,0},{16,28},{20,24},{24,20},{28,16},{1,13},{... | collective-permute-start | bytes 405512 | tf_op jit(solution)/shard_map/ppermute | solution.py:269
  48.9 1.5 %collective-permute-start.4 = (s16[33,16,128]{2,1,0:T(8,128)(2,1)S(1)}, s16[33,16,128]{2,1,0:T(8,128)(2,1)S(1)}, u32[]{:S(2)}, u32[]{:S(2)}) collective-permute-start(s16[33,16,128]{2,1,0:T(8,128)(2,1)S(1)} %get-tuple-element.22), channel_id=1, source_target_pairs={{0,4},{4,0},{8,12},{12,8},{16,20},{20,16},{24,28},{28,24},{1,5},{5... | collective-permute-start | bytes 405512 | tf_op jit(solution)/shard_map/ppermute | solution.py:269
  50.4 0.5 collective-permute-start.5
  50.9 2.6 %collective-permute-start.6 = (s16[33,16,128]{2,1,0:T(8,128)(2,1)S(1)}, s16[33,16,128]{2,1,0:T(8,128)(2,1)S(1)}, u32[]{:S(2)}, u32[]{:S(2)}) collective-permute-start(s16[33,16,128]{2,1,0:T(8,128)(2,1)S(1)} %get-tuple-element.24), channel_id=1, source_target_pairs={{0,16},{4,20},{8,24},{12,28},{16,0},{20,4},{24,8},{28,12},{1,17},{... | collective-permute-start | bytes 405512 | tf_op jit(solution)/shard_map/ppermute | solution.py:269
  53.5 5.3 %collective-permute-start.7 = (s16[33,16,128]{2,1,0:T(8,128)(2,1)S(1)}, s16[33,16,128]{2,1,0:T(8,128)(2,1)S(1)}, u32[]{:S(2)}, u32[]{:S(2)}) collective-permute-start(s16[33,16,128]{2,1,0:T(8,128)(2,1)S(1)} %get-tuple-element.25), channel_id=1, source_target_pairs={{0,20},{4,16},{8,28},{12,24},{16,4},{20,0},{24,12},{28,8},{1,21},{... | collective-permute-start | bytes 405512 | tf_op jit(solution)/shard_map/ppermute | solution.py:269
  58.8 2.1 %collective-permute-start.8 = (s16[33,16,128]{2,1,0:T(8,128)(2,1)S(1)}, s16[33,16,128]{2,1,0:T(8,128)(2,1)S(1)}, u32[]{:S(2)}, u32[]{:S(2)}) collective-permute-start(s16[33,16,128]{2,1,0:T(8,128)(2,1)S(1)} %get-tuple-element.26), channel_id=1, source_target_pairs={{0,24},{4,28},{8,16},{12,20},{16,8},{20,12},{24,0},{28,4},{1,25},{... | collective-permute-start | bytes 405512 | tf_op jit(solution)/shard_map/ppermute | solution.py:269
  60.9 1.5 %collective-permute-start.9 = (s16[33,16,128]{2,1,0:T(8,128)(2,1)S(1)}, s16[33,16,128]{2,1,0:T(8,128)(2,1)S(1)}, u32[]{:S(2)}, u32[]{:S(2)}) collective-permute-start(s16[33,16,128]{2,1,0:T(8,128)(2,1)S(1)} %get-tuple-element.27), channel_id=1, source_target_pairs={{0,28},{4,24},{8,20},{12,16},{16,12},{20,8},{24,4},{28,0},{1,29},{... | collective-permute-start | bytes 405512 | tf_op jit(solution)/shard_map/ppermute | solution.py:269
  62.4 3.1 %collective-permute-start.10 = (s16[33,16,128]{2,1,0:T(8,128)(2,1)S(1)}, s16[33,16,128]{2,1,0:T(8,128)(2,1)S(1)}, u32[]{:S(2)}, u32[]{:S(2)}) collective-permute-start(s16[33,16,128]{2,1,0:T(8,128)(2,1)S(1)} %get-tuple-element.28), channel_id=1, source_target_pairs={{0,12},{4,8},{8,4},{12,0},{16,28},{20,24},{24,20},{28,16},{1,13},{... | collective-permute-start | bytes 405512 | tf_op jit(solution)/shard_map/ppermute | solution.py:269
  65.7 2.9 %tile_sums.2.refs_8_ = f32[64,8,1024]{2,1,0:T(8,128)} custom-call(s32[2]{0:T(128)S(1)} %pad_add_fusion.ids, s32[16]{0:T(128)S(1)} %reshape.7.targets, s32[8]{0:T(128)S(1)} %copy-done.2, s16[33,16,128]{2,1,0:T(8,128)(2,1)S(1)} %collective-permute-done.11.refs_0_, s16[33,16,128]{2,1,0:T(8,128)(2,1)S(1)} %collective-permute-done.12.refs_1_, ...), custom_call_target="tpu_custom_call" | custom-call | flops 2097152 | bytes 2097152 | tf_op jit(solution)/shard_map/tile_sums/pallas_call | solution.py:237
  68.6 3.5 %collective-permute-done.7.refs_3_ = s16[33,16,128]{2,1,0:T(8,128)(2,1)S(1)} collective-permute-done((s16[33,16,128]{2,1,0:T(8,128)(2,1)S(1)}, s16[33,16,128]{2,1,0:T(8,128)(2,1)S(1)}, u32[]{:S(2)}, u32[]{:S(2)}) %collective-permute-start.7) | collective-permute-done | bytes 135200 | tf_op jit(solution)/shard_map/ppermute | solution.py:269
  72.0 3.3 %collective-permute-done.8.refs_4_ = s16[33,16,128]{2,1,0:T(8,128)(2,1)S(1)} collective-permute-done((s16[33,16,128]{2,1,0:T(8,128)(2,1)S(1)}, s16[33,16,128]{2,1,0:T(8,128)(2,1)S(1)}, u32[]{:S(2)}, u32[]{:S(2)}) %collective-permute-start.8) | collective-permute-done | bytes 135200 | tf_op jit(solution)/shard_map/ppermute | solution.py:269
  75.4 1.8 %collective-permute-done.9.refs_5_ = s16[33,16,128]{2,1,0:T(8,128)(2,1)S(1)} collective-permute-done((s16[33,16,128]{2,1,0:T(8,128)(2,1)S(1)}, s16[33,16,128]{2,1,0:T(8,128)(2,1)S(1)}, u32[]{:S(2)}, u32[]{:S(2)}) %collective-permute-start.9) | collective-permute-done | bytes 135200 | tf_op jit(solution)/shard_map/ppermute | solution.py:269
  77.2 2.9 %tile_sums.3 = f32[64,8,1024]{2,1,0:T(8,128)} custom-call(s32[2]{0:T(128)S(1)} %pad_add_fusion.ids, s32[16]{0:T(128)S(1)} %reshape.7.targets, s32[8]{0:T(128)S(1)} %copy-done.2, s16[33,16,128]{2,1,0:T(8,128)(2,1)S(1)} %collective-permute-done.4.refs_0_, s16[33,16,128]{2,1,0:T(8,128)(2,1)S(1)} %collective-permute-done.5.refs_1_, ...), custom_call_target="tpu_custom_call", output_to_operand_aliasing={{}: (11, {})} | custom-call | flops 2097152 | bytes 2097152 | tf_op jit(solution)/shard_map/tile_sums/pallas_call | solution.py:237
  (28 shorter events, 0.7 us)
Async XLA Ops:
  0.0 8.0 %collective-permute-start.1 = (bf16[2,64,4096]{2,1,0:T(8,128)(2,1)}, bf16[2,64,4096]{2,1,0:T(8,128)(2,1)S(1)}, u32[]{:S(2)}, u32[]{:S(2)}) collective-permute-start(bf16[2,64,4096]{2,1,0:T(8,128)(2,1)} %bitcast.3), channel_id=1, source_target_pairs={{0,1},{1,0},{2,3},{3,2},{4,5},{5,4},{6,7},{7,6},{8,9},{9,8},{10,11... | collective-permute-start | bytes 3145736 | tf_op jit(solution)/shard_map/ppermute | solution.py:269
  0.0 1.2 %copy-start = (bf16[128,1,4096]{2,0,1:T(8,128)(2,1)S(1)}, bf16[128,1,4096]{2,0,1:T(8,128)(2,1)}, u32[]{:S(2)}) copy-start(bf16[128,1,4096]{2,0,1:T(8,128)(2,1)} %param.4) | copy-start | bytes 3145732
  1.3 14.4 %collective-permute-start = (bf16[2,32,4096]{2,1,0:T(8,128)(2,1)S(1)}, bf16[2,32,4096]{2,1,0:T(8,128)(2,1)S(1)}, u32[]{:S(2)}, u32[]{:S(2)}) collective-permute-start(bf16[2,32,4096]{2,1,0:T(8,128)(2,1)S(1)} %picked_rows.3), channel_id=1, source_target_pairs={{0,2},{1,3},{2,0},{3,1},{4,6},{5,7},{6,4},{7,5},{8,10},{9,11},{10,... | collective-permute-start | bytes 1572872 | tf_op jit(solution)/shard_map/ppermute | solution.py:269
  1.9 6.0 %copy-start.1 = (bf16[128,1,4096]{2,0,1:T(8,128)(2,1)S(1)}, bf16[128,1,4096]{2,0,1:T(8,128)(2,1)}, u32[]{:S(2)}) copy-start(bf16[128,1,4096]{2,0,1:T(8,128)(2,1)} %param.4) | copy-start | bytes 3145732
  15.7 2.0 %collective-permute-start.2 = (bf16[2,32,4096]{2,1,0:T(8,128)(2,1)S(1)}, bf16[2,32,4096]{2,1,0:T(8,128)(2,1)S(1)}, u32[]{:S(2)}, u32[]{:S(2)}) collective-permute-start(bf16[2,32,4096]{2,1,0:T(8,128)(2,1)S(1)} %picked_rows.4), channel_id=1, source_target_pairs={{0,1},{1,0},{2,3},{3,2},{4,5},{5,4},{6,7},{7,6},{8,9},{9,8},{10,11... | collective-permute-start | bytes 1572872 | tf_op jit(solution)/shard_map/ppermute | solution.py:269
  16.1 25.6 %collective-permute-start.3 = (bf16[4,32,4096]{2,1,0:T(8,128)(2,1)S(1)}, bf16[4,32,4096]{2,1,0:T(8,128)(2,1)S(1)}, u32[]{:S(2)}, u32[]{:S(2)}) collective-permute-start(bf16[4,32,4096]{2,1,0:T(8,128)(2,1)S(1)} %picked_rows.5), channel_id=1, source_target_pairs={{0,2},{1,3},{2,0},{3,1},{4,6},{5,7},{6,4},{7,5},{8,10},{9,11},{10,... | collective-permute-start | bytes 3145736 | tf_op jit(solution)/shard_map/ppermute | solution.py:269
  21.4 25.5 %collective-permute-start.11 = (s16[33,16,128]{2,1,0:T(8,128)(2,1)S(1)}, s16[33,16,128]{2,1,0:T(8,128)(2,1)S(1)}, u32[]{:S(2)}, u32[]{:S(2)}) collective-permute-start(s16[33,16,128]{2,1,0:T(8,128)(2,1)S(1)} %get-tuple-element.30), channel_id=1, source_target_pairs={{0,16},{4,20},{8,24},{12,28},{16,0},{20,4},{24,8},{28,12},{1,17},{... | collective-permute-start | bytes 405512 | tf_op jit(solution)/shard_map/ppermute | solution.py:269
  24.0 23.4 %collective-permute-start.12 = (s16[33,16,128]{2,1,0:T(8,128)(2,1)S(1)}, s16[33,16,128]{2,1,0:T(8,128)(2,1)S(1)}, u32[]{:S(2)}, u32[]{:S(2)}) collective-permute-start(s16[33,16,128]{2,1,0:T(8,128)(2,1)S(1)} %get-tuple-element.31), channel_id=1, source_target_pairs={{0,20},{4,16},{8,28},{12,24},{16,4},{20,0},{24,12},{28,8},{1,21},{... | collective-permute-start | bytes 405512 | tf_op jit(solution)/shard_map/ppermute | solution.py:269
  25.3 23.6 %collective-permute-start.13 = (s16[33,16,128]{2,1,0:T(8,128)(2,1)S(1)}, s16[33,16,128]{2,1,0:T(8,128)(2,1)S(1)}, u32[]{:S(2)}, u32[]{:S(2)}) collective-permute-start(s16[33,16,128]{2,1,0:T(8,128)(2,1)S(1)} %get-tuple-element.32), channel_id=1, source_target_pairs={{0,24},{4,28},{8,16},{12,20},{16,8},{20,12},{24,0},{28,4},{1,25},{... | collective-permute-start | bytes 405512 | tf_op jit(solution)/shard_map/ppermute | solution.py:269
  26.9 23.6 %collective-permute-start.14 = (s16[33,16,128]{2,1,0:T(8,128)(2,1)S(1)}, s16[33,16,128]{2,1,0:T(8,128)(2,1)S(1)}, u32[]{:S(2)}, u32[]{:S(2)}) collective-permute-start(s16[33,16,128]{2,1,0:T(8,128)(2,1)S(1)} %get-tuple-element.33), channel_id=1, source_target_pairs={{0,28},{4,24},{8,20},{12,16},{16,12},{20,8},{24,4},{28,0},{1,29},{... | collective-permute-start | bytes 405512 | tf_op jit(solution)/shard_map/ppermute | solution.py:269
  41.7 23.8 %copy-start.3 = (s32[8,2]{0,1:T(2,128)S(1)}, s32[8,2]{0,1:T(2,128)}, u32[]{:S(2)}) copy-start(s32[8,2]{0,1:T(2,128)} %param.6) | copy-start | bytes 196
  41.7 24.0 %copy-start.2 = (s32[8]{0:T(128)S(1)}, s32[8]{0:T(128)}, u32[]{:S(2)}) copy-start(s32[8]{0:T(128)} %counts.3) | copy-start | bytes 100
  41.7 9.2 %collective-permute-start.15 = (s16[33,16,128]{2,1,0:T(8,128)(2,1)S(1)}, s16[33,16,128]{2,1,0:T(8,128)(2,1)S(1)}, u32[]{:S(2)}, u32[]{:S(2)}) collective-permute-start(s16[33,16,128]{2,1,0:T(8,128)(2,1)S(1)} %get-tuple-element.34), channel_id=1, source_target_pairs={{0,4},{4,0},{8,12},{12,8},{16,20},{20,16},{24,28},{28,24},{1,5},{5... | collective-permute-start | bytes 405512 | tf_op jit(solution)/shard_map/ppermute | solution.py:269
  46.9 6.6 %collective-permute-start.16 = (s16[33,16,128]{2,1,0:T(8,128)(2,1)S(1)}, s16[33,16,128]{2,1,0:T(8,128)(2,1)S(1)}, u32[]{:S(2)}, u32[]{:S(2)}) collective-permute-start(s16[33,16,128]{2,1,0:T(8,128)(2,1)S(1)} %get-tuple-element.35), channel_id=1, source_target_pairs={{0,8},{4,12},{8,0},{12,4},{16,24},{20,28},{24,16},{28,20},{1,9},{5... | collective-permute-start | bytes 405512 | tf_op jit(solution)/shard_map/ppermute | solution.py:269
  47.4 11.4 %collective-permute-start.17 = (s16[33,16,128]{2,1,0:T(8,128)(2,1)S(1)}, s16[33,16,128]{2,1,0:T(8,128)(2,1)S(1)}, u32[]{:S(2)}, u32[]{:S(2)}) collective-permute-start(s16[33,16,128]{2,1,0:T(8,128)(2,1)S(1)} %get-tuple-element.36), channel_id=1, source_target_pairs={{0,12},{4,8},{8,4},{12,0},{16,28},{20,24},{24,20},{28,16},{1,13},{... | collective-permute-start | bytes 405512 | tf_op jit(solution)/shard_map/ppermute | solution.py:269
  48.9 12.0 %collective-permute-start.4 = (s16[33,16,128]{2,1,0:T(8,128)(2,1)S(1)}, s16[33,16,128]{2,1,0:T(8,128)(2,1)S(1)}, u32[]{:S(2)}, u32[]{:S(2)}) collective-permute-start(s16[33,16,128]{2,1,0:T(8,128)(2,1)S(1)} %get-tuple-element.22), channel_id=1, source_target_pairs={{0,4},{4,0},{8,12},{12,8},{16,20},{20,16},{24,28},{28,24},{1,5},{5... | collective-permute-start | bytes 405512 | tf_op jit(solution)/shard_map/ppermute | solution.py:269
  50.4 11.9 %collective-permute-start.5 = (s16[33,16,128]{2,1,0:T(8,128)(2,1)S(1)}, s16[33,16,128]{2,1,0:T(8,128)(2,1)S(1)}, u32[]{:S(2)}, u32[]{:S(2)}) collective-permute-start(s16[33,16,128]{2,1,0:T(8,128)(2,1)S(1)} %get-tuple-element.23), channel_id=1, source_target_pairs={{0,8},{4,12},{8,0},{12,4},{16,24},{20,28},{24,16},{28,20},{1,9},{5... | collective-permute-start | bytes 405512 | tf_op jit(solution)/shard_map/ppermute | solution.py:269
  50.9 17.7 %collective-permute-start.6 = (s16[33,16,128]{2,1,0:T(8,128)(2,1)S(1)}, s16[33,16,128]{2,1,0:T(8,128)(2,1)S(1)}, u32[]{:S(2)}, u32[]{:S(2)}) collective-permute-start(s16[33,16,128]{2,1,0:T(8,128)(2,1)S(1)} %get-tuple-element.24), channel_id=1, source_target_pairs={{0,16},{4,20},{8,24},{12,28},{16,0},{20,4},{24,8},{28,12},{1,17},{... | collective-permute-start | bytes 405512 | tf_op jit(solution)/shard_map/ppermute | solution.py:269
  53.5 18.6 %collective-permute-start.7 = (s16[33,16,128]{2,1,0:T(8,128)(2,1)S(1)}, s16[33,16,128]{2,1,0:T(8,128)(2,1)S(1)}, u32[]{:S(2)}, u32[]{:S(2)}) collective-permute-start(s16[33,16,128]{2,1,0:T(8,128)(2,1)S(1)} %get-tuple-element.25), channel_id=1, source_target_pairs={{0,20},{4,16},{8,28},{12,24},{16,4},{20,0},{24,12},{28,8},{1,21},{... | collective-permute-start | bytes 405512 | tf_op jit(solution)/shard_map/ppermute | solution.py:269
  58.8 16.6 %collective-permute-start.8 = (s16[33,16,128]{2,1,0:T(8,128)(2,1)S(1)}, s16[33,16,128]{2,1,0:T(8,128)(2,1)S(1)}, u32[]{:S(2)}, u32[]{:S(2)}) collective-permute-start(s16[33,16,128]{2,1,0:T(8,128)(2,1)S(1)} %get-tuple-element.26), channel_id=1, source_target_pairs={{0,24},{4,28},{8,16},{12,20},{16,8},{20,12},{24,0},{28,4},{1,25},{... | collective-permute-start | bytes 405512 | tf_op jit(solution)/shard_map/ppermute | solution.py:269
  60.9 16.3 %collective-permute-start.9 = (s16[33,16,128]{2,1,0:T(8,128)(2,1)S(1)}, s16[33,16,128]{2,1,0:T(8,128)(2,1)S(1)}, u32[]{:S(2)}, u32[]{:S(2)}) collective-permute-start(s16[33,16,128]{2,1,0:T(8,128)(2,1)S(1)} %get-tuple-element.27), channel_id=1, source_target_pairs={{0,28},{4,24},{8,20},{12,16},{16,12},{20,8},{24,4},{28,0},{1,29},{... | collective-permute-start | bytes 405512 | tf_op jit(solution)/shard_map/ppermute | solution.py:269
  62.4 14.8 %collective-permute-start.10 = (s16[33,16,128]{2,1,0:T(8,128)(2,1)S(1)}, s16[33,16,128]{2,1,0:T(8,128)(2,1)S(1)}, u32[]{:S(2)}, u32[]{:S(2)}) collective-permute-start(s16[33,16,128]{2,1,0:T(8,128)(2,1)S(1)} %get-tuple-element.28), channel_id=1, source_target_pairs={{0,12},{4,8},{8,4},{12,0},{16,28},{20,24},{24,20},{28,16},{1,13},{... | collective-permute-start | bytes 405512 | tf_op jit(solution)/shard_map/ppermute | solution.py:269

commit v3 on v2

--- a/solution.py
+++ b/solution.py
@@ -195,29 +195,35 @@
     )(ids, *after, *pieces, *early, integrals)
 
 
-def sum_kernel(slots, plan, start, rows, cols, ids, targets, counts, *refs):
-    out, total, turned, done = refs[-4:]
+def sum_kernel(slots, plan, start, rows, cols, begun, last, ids, targets, counts, *refs):
+    out, total, turned, done = refs[-4:] if last else (None, refs[-1], None, None)
     me = ids[0]
     groups, lanes = rows // 16, cols // 128
     tiles = slots * groups * lanes + 1
-    total[...] = jnp.zeros_like(total)
-    lane = lax.broadcasted_iota(jnp.int32, (16, 128), 1)
-    for index, bits, at in plan:
+    total[...] = refs[len(plan)][...] if begun else jnp.zeros_like(total)
+    scales = []
+    for index, _, at in plan:
+        codes = refs[index][at + tiles - 1].astype(jnp.int32).astype(jnp.float32)
+        exponents = jnp.exp2(jnp.clip(codes, -125.0, 125.0))
+        scales.append(exponents * (pltpu.roll(codes, 127, 1) * (1.0 / (TOP * MANT))))
+    for (index, bits, at), scale in zip(plan, scales):
         panel = me ^ bits
-        codes = refs[index][at + tiles - 1].astype(jnp.int32)
         for j in range(slots):
 
             @pl.when(j < counts[panel])
             def add():
                 tile = targets[panel * slots + j]
-                for g in range(groups):
-                    spot = (j * groups + g) * 2
-                    exponent = jnp.sum(jnp.where(lane == spot, codes, 0).astype(jnp.float32), axis=1, keepdims=True)
-                    mantissa = jnp.sum(jnp.where(lane == spot + 1, codes, 0).astype(jnp.float32), axis=1, keepdims=True)
-                    scale = jnp.exp2(exponent) * (mantissa * (1.0 / (TOP * MANT)))
-                    for t in range(lanes):
-                        value = refs[index][at + (j * groups + g) * lanes + t].astype(jnp.int32).astype(jnp.float32)
-                        total[tile, g * 16 : g * 16 + 16, t * 128 : t * 128 + 128] += value * scale
+                spots = [(slice(g * 16, g * 16 + 16), slice(t * 128, t * 128 + 128)) for g in range(groups) for t in range(lanes)]
+                columns = [scale[:, (j * groups + g) * 2 : (j * groups + g) * 2 + 1] for g in range(groups)]
+                values = []
+                for i, (r, c) in enumerate(spots):
+                    value = refs[index][at + j * groups * lanes + i].astype(jnp.int32).astype(jnp.float32)
+                    values.append(total[tile, r, c] + value * columns[i // lanes])
+                for value, (r, c) in zip(values, spots):
+                    total[tile, r, c] = value
+
+    if not last:
+        return
     copies = []
     for g in range(rows // 8):
         part = slice(g * 8, g * 8 + 8)
@@ -230,29 +236,30 @@
         copy.wait()
 
 
-def summed(ids, targets, counts, given, plan, held, start, rows, cols, height):
+def summed(ids, targets, counts, given, plan, begun, held, last, start, rows, cols, height):
     pairs, slots = targets.shape
-    extra = [] if held is None else [held]
     smem, vmem = pl.BlockSpec(memory_space=pltpu.SMEM), pl.BlockSpec(memory_space=pltpu.VMEM)
-    return pl.pallas_call(
-        functools.partial(sum_kernel, slots, plan, start, rows, cols),
-        out_shape=jax.ShapeDtypeStruct((height, pairs, cols), jnp.float32),
-        in_specs=[smem] * 3 + [vmem] * len(given) + [pl.BlockSpec(memory_space=pl.ANY)] * len(extra),
-        out_specs=pl.BlockSpec(memory_space=pl.ANY),
-        scratch_shapes=[
-            pltpu.VMEM((pairs, rows, cols), jnp.float32),
-            pltpu.VMEM((rows, pairs, cols), jnp.float32),
-            pltpu.SemaphoreType.DMA((rows // 8,)),
-        ],
-        input_output_aliases={3 + len(given): 0} if extra else {},
+    scratch = [
+        pltpu.VMEM((pairs, rows, cols), jnp.float32),
+        pltpu.VMEM((rows, pairs, cols), jnp.float32),
+        pltpu.SemaphoreType.DMA((rows // 8,)),
+    ]
+    shape = (height, pairs, cols) if last else (pairs, rows, cols)
+    return pl.pallas_call(
+        functools.partial(sum_kernel, slots, plan, start, rows, cols, len(begun) > 0, last),
+        out_shape=jax.ShapeDtypeStruct(shape, jnp.float32),
+        in_specs=[smem] * 3 + [vmem] * (len(given) + len(begun)) + [pl.BlockSpec(memory_space=pl.ANY)] * len(held),
+        out_specs=pl.BlockSpec(memory_space=pl.ANY) if last else vmem,
+        scratch_shapes=scratch if last else [],
+        input_output_aliases={3 + len(given) + len(begun): 0} if held else {},
         compiler_params=pltpu.CompilerParams(vmem_limit_bytes=32 * MIB),
         cost_estimate=pl.CostEstimate(
-            flops=4 * pairs * slots * rows * cols,
-            bytes_accessed=2 * pairs * slots * rows * cols + 4 * pairs * rows * cols,
+            flops=4 * len(given) * slots * rows * cols,
+            bytes_accessed=2 * len(given) * slots * rows * cols + 4 * pairs * rows * cols,
             transcendentals=0,
         ),
         name="tile_sums",
-    )(ids, targets.reshape(-1), counts, *given, *extra)
+    )(ids, targets.reshape(-1), counts, *given, *begun, *held)
 
 
 def on_device(amplitudes, integrals, targets, counts):
@@ -286,13 +293,26 @@
         sent = far_products(ids, pieces, early, kept, wide, share, waits)
         waits = [sent[0]]
         crossing, others = [*range(wide // 2, wide)], [*range(2, wide // 2)]
-        order = [1, *others[:1], *crossing, *others[1:]] if rows == height - start else [*crossing, 1, *others]
+        order = [*crossing, 1, *others]
+        if start:
+            order = [crossing[0], 1, crossing[1], *others[:1], *crossing[2:], *others[1:]]
         given = [across(sent[s], "wide", wide, s) for s in order] + [sent[0]]
         received.append((given, tuple((i, s, 0) for i, s in enumerate([*order, 0]))))
-    held = None
+    held = []
     for (given, plan), start, rows in zip(received, starts, parts):
-        held = summed(ids, targets, counts, given, plan, held, start, rows, cols, height)
-    return held
+        begun = []
+        if start:
+            ahead = wide // 2
+            first = [*given[:ahead], given[-1]]
+            order = [s for _, s, _ in plan]
+            marks = [*order[:ahead], 0]
+            begun = [
+                summed(ids, targets, counts, first, tuple((i, s, 0) for i, s in enumerate(marks)), [], [], False, start, rows, cols, height)
+            ]
+            given, marks = given[ahead:-1], order[ahead:-1]
+            plan = tuple((i, s, 0) for i, s in enumerate(marks))
+        held = [summed(ids, targets, counts, given, plan, begun, held, True, start, rows, cols, height)]
+    return held[0]
 
 
 def solution(mesh):

time: 80.2 us -> 77.7 us (0.969)
  the two profiles are of different devices: /device:TPU:10 before, /device:TPU:0 now
where the time goes in v3:
time: 77.7 us; the launch traced here: 77.5 us
  starting transfers between devices  27.9 us (36%)
  Pallas kernels  25.2 us (32%)
  waiting for transfers between devices  22.4 us (29%)
  local copies, waits for them, and re-layouts  1.67 us (2%)
    ppermute x18, starting transfers between devices, across(): return lax.ppermute(array, axis, [(i, i ^ bits) for i in range(size)])  27.9 us
    ppermute x18, waiting for transfers between devices, across(): return lax.ppermute(array, axis, [(i, i ^ bits) for i in range(size)])  22.4 us
    pallas_call x2, Pallas kernels, far_products(): pl.pallas_call(functools.partial(far_kernel, slots, wide, count, share, r...  7.23 us
    pallas_call x3, Pallas kernels, summed(): pl.pallas_call(functools.partial(sum_kernel, slots, plan, start, rows, co...  5.97 us
    pallas_call x2, Pallas kernels, near_products(): pl.pallas_call(functools.partial(near_kernel, slots, share, len(after)),...  5.93 us
    pallas_call x1, Pallas kernels, staged(): pl.pallas_call(stage_kernel, out_shape=pltpu.VMEM(integrals.shape, integr...  5.87 us
  transfers between devices with their start and end apart: 18, of which 7 were waited for; matrix products, arithmetic and copies ran while one was open for 1% of the time, Pallas kernels for 30%

profile of v3, /device:TPU:0, one launch (start us, length us, event | category | flops | bytes accessed | tf_op | source)
XLA Modules:
  0.0 77.5 jit_solution(1744257073498426255)
XLA Ops:
  0.0 0.5 collective-permute-start.1
  0.5 1.2 %copy-done = bf16[128,1,4096]{2,0,1:T(8,128)(2,1)S(1)} copy-done((bf16[128,1,4096]{2,0,1:T(8,128)(2,1)S(1)}, bf16[128,1,4096]{2,0,1:T(8,128)(2,1)}, u32[]{:S(2)}) %copy-start) | copy-done | bytes 1048600
  1.7 2.6 %collective-permute-start = (bf16[2,32,4096]{2,1,0:T(8,128)(2,1)S(1)}, bf16[2,32,4096]{2,1,0:T(8,128)(2,1)S(1)}, u32[]{:S(2)}, u32[]{:S(2)}) collective-permute-start(bf16[2,32,4096]{2,1,0:T(8,128)(2,1)S(1)} %picked_rows.3), channel_id=1, source_target_pairs={{0,2},{1,3},{2,0},{3,1},{4,6},{5,7},{6,4},{7,5},{8,10},{9,11},{10,... | collective-permute-start | bytes 1572872 | tf_op jit(solution)/shard_map/ppermute | solution.py:276
  4.3 5.9 %staged_integrals.1.refs_2_.refs_0_.refs_3_ = bf16[1,2,4096,1024]{3,2,1,0:T(8,128)(2,1)S(1)} custom-call(bf16[1,2,4096,1024]{3,2,1,0:T(8,128)(2,1)} %source.1), custom_call_target="tpu_custom_call" | custom-call | tf_op jit(solution)/shard_map/staged_integrals/pallas_call | solution.py:84
  10.2 0.1 copy-done.1
  10.5 3.0 %near_products.2.refs_1_.refs_2_ = s16[4,33,16,128]{3,2,1,0:T(8,128)(2,1)S(1)} custom-call(bf16[2,32,4096]{2,1,0:T(8,128)(2,1)S(1)} %get-tuple-element.38.refs_0_, bf16[2,32,4096]{2,1,0:T(8,128)(2,1)S(1)} %get-tuple-element.40.refs_1_, bf16[1,2,4096,1024]{3,2,1,0:T(8,128)(2,1)S(1)} %staged_integrals.1.refs_2_.refs_0_.refs_3_), custom_call_target="tpu_custom_call" | custom-call | flops 17179869184 | bytes 1048576 | tf_op jit(solution)/shard_map/near_products/pallas_call | solution.py:151
  13.4 3.4 %collective-permute-done.source.refs_0_ = bf16[2,32,4096]{2,1,0:T(8,128)(2,1)S(1)} collective-permute-done((bf16[2,32,4096]{2,1,0:T(8,128)(2,1)S(1)}, bf16[2,32,4096]{2,1,0:T(8,128)(2,1)S(1)}, u32[]{:S(2)}, u32[]{:S(2)}) %collective-permute-start) | collective-permute-done | bytes 524320 | tf_op jit(solution)/shard_map/ppermute | solution.py:276
  17.1 0.1 pad_maximum_fusion.source
  17.3 1.8 %collective-permute-start.3 = (bf16[4,32,4096]{2,1,0:T(8,128)(2,1)S(1)}, bf16[4,32,4096]{2,1,0:T(8,128)(2,1)S(1)}, u32[]{:S(2)}, u32[]{:S(2)}) collective-permute-start(bf16[4,32,4096]{2,1,0:T(8,128)(2,1)S(1)} %picked_rows.5), channel_id=1, source_target_pairs={{0,2},{1,3},{2,0},{3,1},{4,6},{5,7},{6,4},{7,5},{8,10},{9,11},{10,... | collective-permute-start | bytes 3145736 | tf_op jit(solution)/shard_map/ppermute | solution.py:276
  19.1 3.6 %far_products.2 = (s16[33,16,128]{2,1,0:T(8,128)(2,1)S(1)}, s16[33,16,128]{2,1,0:T(8,128)(2,1)S(1)}, s16[33,16,128]{2,1,0:T(8,128)(2,1)S(1)}, s16[33,16,128]{2,1...) custom-call(s32[2]{0:T(128)S(1)} %pad_add_fusion.ids, ...), custom_call_target="tpu_custom_call" | custom-call | flops 17179869184 | bytes 1048576 | tf_op jit(solution)/shard_map/far_products/pallas_call | solution.py:176
  22.7 2.7 %collective-permute-start.11 = (s16[33,16,128]{2,1,0:T(8,128)(2,1)S(1)}, s16[33,16,128]{2,1,0:T(8,128)(2,1)S(1)}, u32[]{:S(2)}, u32[]{:S(2)}) collective-permute-start(s16[33,16,128]{2,1,0:T(8,128)(2,1)S(1)} %get-tuple-element.30), channel_id=1, source_target_pairs={{0,16},{4,20},{8,24},{12,28},{16,0},{20,4},{24,8},{28,12},{1,17},{... | collective-permute-start | bytes 405512 | tf_op jit(solution)/shard_map/ppermute | solution.py:276
  25.5 1.3 %collective-permute-start.12 = (s16[33,16,128]{2,1,0:T(8,128)(2,1)S(1)}, s16[33,16,128]{2,1,0:T(8,128)(2,1)S(1)}, u32[]{:S(2)}, u32[]{:S(2)}) collective-permute-start(s16[33,16,128]{2,1,0:T(8,128)(2,1)S(1)} %get-tuple-element.31), channel_id=1, source_target_pairs={{0,20},{4,16},{8,28},{12,24},{16,4},{20,0},{24,12},{28,8},{1,21},{... | collective-permute-start | bytes 405512 | tf_op jit(solution)/shard_map/ppermute | solution.py:276
  26.7 3.6 %collective-permute-start.13 = (s16[33,16,128]{2,1,0:T(8,128)(2,1)S(1)}, s16[33,16,128]{2,1,0:T(8,128)(2,1)S(1)}, u32[]{:S(2)}, u32[]{:S(2)}) collective-permute-start(s16[33,16,128]{2,1,0:T(8,128)(2,1)S(1)} %get-tuple-element.32), channel_id=1, source_target_pairs={{0,24},{4,28},{8,16},{12,20},{16,8},{20,12},{24,0},{28,4},{1,25},{... | collective-permute-start | bytes 405512 | tf_op jit(solution)/shard_map/ppermute | solution.py:276
  30.4 3.0 %near_products.3.refs_2_ = s16[4,33,16,128]{3,2,1,0:T(8,128)(2,1)S(1)} custom-call(s16[33,16,128]{2,1,0:T(8,128)(2,1)S(1)} %get-tuple-element.21.refs_0_.refs_7_, bf16[2,32,4096]{2,1,0:T(8,128)(2,1)S(1)} %get-tuple-element.37.refs_1_, bf16[2,32,4096]{2,1,0:T(8,128)(2,1)S(1)} %get-tuple-element.39.refs_2_, ...), custom_call_target="tpu_custom_call" | custom-call | flops 17179869184 | bytes 1048576 | tf_op jit(solution)/shard_map/near_products/pallas_call | solution.py:151
  33.4 9.5 %collective-permute-done.3.refs_1_ = bf16[4,32,4096]{2,1,0:T(8,128)(2,1)S(1)} collective-permute-done((bf16[4,32,4096]{2,1,0:T(8,128)(2,1)S(1)}, bf16[4,32,4096]{2,1,0:T(8,128)(2,1)S(1)}, u32[]{:S(2)}, u32[]{:S(2)}) %collective-permute-start.3) | collective-permute-done | bytes 1048608 | tf_op jit(solution)/shard_map/ppermute | solution.py:276
  42.9 1.8 %collective-permute-start.15 = (s16[33,16,128]{2,1,0:T(8,128)(2,1)S(1)}, s16[33,16,128]{2,1,0:T(8,128)(2,1)S(1)}, u32[]{:S(2)}, u32[]{:S(2)}) collective-permute-start(s16[33,16,128]{2,1,0:T(8,128)(2,1)S(1)} %get-tuple-element.34), channel_id=1, source_target_pairs={{0,4},{4,0},{8,12},{12,8},{16,20},{20,16},{24,28},{28,24},{1,5},{5... | collective-permute-start | bytes 405512 | tf_op jit(solution)/shard_map/ppermute | solution.py:276
  44.7 3.6 %far_products.3 = (s16[33,16,128]{2,1,0:T(8,128)(2,1)S(1)}, s16[33,16,128]{2,1,0:T(8,128)(2,1)S(1)}, s16[33,16,128]{2,1,0:T(8,128)(2,1)S(1)}, s16[33,16,128]{2,1...) custom-call(s32[2]{0:T(128)S(1)} %pad_add_fusion.ids, ...), custom_call_target="tpu_custom_call" | custom-call | flops 17179869184 | bytes 1048576 | tf_op jit(solution)/shard_map/far_products/pallas_call | solution.py:176
  48.3 1.6 %collective-permute-start.16 = (s16[33,16,128]{2,1,0:T(8,128)(2,1)S(1)}, s16[33,16,128]{2,1,0:T(8,128)(2,1)S(1)}, u32[]{:S(2)}, u32[]{:S(2)}) collective-permute-start(s16[33,16,128]{2,1,0:T(8,128)(2,1)S(1)} %get-tuple-element.35), channel_id=1, source_target_pairs={{0,8},{4,12},{8,0},{12,4},{16,24},{20,28},{24,16},{28,20},{1,9},{5... | collective-permute-start | bytes 405512 | tf_op jit(solution)/shard_map/ppermute | solution.py:276
  50.0 0.1 collective-permute-start.17
  50.1 2.8 %collective-permute-start.7 = (s16[33,16,128]{2,1,0:T(8,128)(2,1)S(1)}, s16[33,16,128]{2,1,0:T(8,128)(2,1)S(1)}, u32[]{:S(2)}, u32[]{:S(2)}) collective-permute-start(s16[33,16,128]{2,1,0:T(8,128)(2,1)S(1)} %get-tuple-element.25), channel_id=1, source_target_pairs={{0,16},{4,20},{8,24},{12,28},{16,0},{20,4},{24,8},{28,12},{1,17},{... | collective-permute-start | bytes 405512 | tf_op jit(solution)/shard_map/ppermute | solution.py:276
  52.9 1.5 %collective-permute-start.8 = (s16[33,16,128]{2,1,0:T(8,128)(2,1)S(1)}, s16[33,16,128]{2,1,0:T(8,128)(2,1)S(1)}, u32[]{:S(2)}, u32[]{:S(2)}) collective-permute-start(s16[33,16,128]{2,1,0:T(8,128)(2,1)S(1)} %get-tuple-element.26), channel_id=1, source_target_pairs={{0,4},{4,0},{8,12},{12,8},{16,20},{20,16},{24,28},{28,24},{1,5},{5... | collective-permute-start | bytes 405512 | tf_op jit(solution)/shard_map/ppermute | solution.py:276
  54.5 0.3 collective-permute-start.9
  54.8 4.8 %collective-permute-done.16.refs_5_ = s16[33,16,128]{2,1,0:T(8,128)(2,1)S(1)} collective-permute-done((s16[33,16,128]{2,1,0:T(8,128)(2,1)S(1)}, s16[33,16,128]{2,1,0:T(8,128)(2,1)S(1)}, u32[]{:S(2)}, u32[]{:S(2)}) %collective-permute-start.16) | collective-permute-done | bytes 135200 | tf_op jit(solution)/shard_map/ppermute | solution.py:276
  59.6 1.1 %collective-permute-done.17.refs_6_ = s16[33,16,128]{2,1,0:T(8,128)(2,1)S(1)} collective-permute-done((s16[33,16,128]{2,1,0:T(8,128)(2,1)S(1)}, s16[33,16,128]{2,1,0:T(8,128)(2,1)S(1)}, u32[]{:S(2)}, u32[]{:S(2)}) %collective-permute-start.17) | collective-permute-done | bytes 135200 | tf_op jit(solution)/shard_map/ppermute | solution.py:276
  60.8 2.7 %collective-permute-start.4 = (s16[33,16,128]{2,1,0:T(8,128)(2,1)S(1)}, s16[33,16,128]{2,1,0:T(8,128)(2,1)S(1)}, u32[]{:S(2)}, u32[]{:S(2)}) collective-permute-start(s16[33,16,128]{2,1,0:T(8,128)(2,1)S(1)} %get-tuple-element.22), channel_id=1, source_target_pairs={{0,24},{4,28},{8,16},{12,20},{16,8},{20,12},{24,0},{28,4},{1,25},{... | collective-permute-start | bytes 405512 | tf_op jit(solution)/shard_map/ppermute | solution.py:276
  63.4 4.4 %collective-permute-start.5 = (s16[33,16,128]{2,1,0:T(8,128)(2,1)S(1)}, s16[33,16,128]{2,1,0:T(8,128)(2,1)S(1)}, u32[]{:S(2)}, u32[]{:S(2)}) collective-permute-start(s16[33,16,128]{2,1,0:T(8,128)(2,1)S(1)} %get-tuple-element.23), channel_id=1, source_target_pairs={{0,28},{4,24},{8,20},{12,16},{16,12},{20,8},{24,4},{28,0},{1,29},{... | collective-permute-start | bytes 405512 | tf_op jit(solution)/shard_map/ppermute | solution.py:276
  68.0 2.7 %tile_sums.4.refs_4_ = f32[64,8,1024]{2,1,0:T(8,128)} custom-call(s32[2]{0:T(128)S(1)} %pad_add_fusion.ids, s32[16]{0:T(128)S(1)} %reshape.8.targets, s32[8]{0:T(128)S(1)} %copy-done.2, s16[33,16,128]{2,1,0:T(8,128)(2,1)S(1)} %collective-permute-done.11.refs_0_, s16[33,16,128]{2,1,0:T(8,128)(2,1)S(1)} %collective-permute-done.12.refs_1_, ...), custom_call_target="tpu_custom_call" | custom-call | flops 2097152 | bytes 2097152 | tf_op jit(solution)/shard_map/tile_sums/pallas_call | solution.py:248
  70.7 0.5 collective-permute-done.9.refs_2_
  71.2 1.2 %tile_sums.3.refs_3_ = f32[8,32,1024]{2,1,0:T(8,128)S(1)} custom-call(s32[2]{0:T(128)S(1)} %pad_add_fusion.ids, s32[16]{0:T(128)S(1)} %reshape.8.targets, s32[8]{0:T(128)S(1)} %copy-done.2, s16[33,16,128]{2,1,0:T(8,128)(2,1)S(1)} %collective-permute-done.7.refs_0_, s16[33,16,128]{2,1,0:T(8,128)(2,1)S(1)} %collective-permute-done.8.refs_1_, ...), custom_call_target="tpu_custom_call" | custom-call | flops 1310720 | bytes 1703936 | tf_op jit(solution)/shard_map/tile_sums/pallas_call | solution.py:248
  72.4 1.9 %collective-permute-done.5.refs_1_ = s16[33,16,128]{2,1,0:T(8,128)(2,1)S(1)} collective-permute-done((s16[33,16,128]{2,1,0:T(8,128)(2,1)S(1)}, s16[33,16,128]{2,1,0:T(8,128)(2,1)S(1)}, u32[]{:S(2)}, u32[]{:S(2)}) %collective-permute-start.5) | collective-permute-done | bytes 135200 | tf_op jit(solution)/shard_map/ppermute | solution.py:276
  74.3 1.1 %collective-permute-done.6.refs_2_ = s16[33,16,128]{2,1,0:T(8,128)(2,1)S(1)} collective-permute-done((s16[33,16,128]{2,1,0:T(8,128)(2,1)S(1)}, s16[33,16,128]{2,1,0:T(8,128)(2,1)S(1)}, u32[]{:S(2)}, u32[]{:S(2)}) %collective-permute-start.6) | collective-permute-done | bytes 135200 | tf_op jit(solution)/shard_map/ppermute | solution.py:276
  75.4 2.1 %tile_sums.5 = f32[64,8,1024]{2,1,0:T(8,128)} custom-call(s32[2]{0:T(128)S(1)} %pad_add_fusion.ids, s32[16]{0:T(128)S(1)} %reshape.8.targets, s32[8]{0:T(128)S(1)} %copy-done.2, s16[33,16,128]{2,1,0:T(8,128)(2,1)S(1)} %collective-permute-done.4.refs_0_, s16[33,16,128]{2,1,0:T(8,128)(2,1)S(1)} %collective-permute-done.5.refs_1_, ...), custom_call_target="tpu_custom_call", output_to_operand_aliasing={{}: (7, {})} | custom-call | flops 786432 | bytes 1441792 | tf_op jit(solution)/shard_map/tile_sums/pallas_call | solution.py:248
  (29 shorter events, 0.8 us)
Async XLA Ops:
  0.0 10.4 %collective-permute-start.1 = (bf16[2,64,4096]{2,1,0:T(8,128)(2,1)}, bf16[2,64,4096]{2,1,0:T(8,128)(2,1)S(1)}, u32[]{:S(2)}, u32[]{:S(2)}) collective-permute-start(bf16[2,64,4096]{2,1,0:T(8,128)(2,1)} %bitcast.3), channel_id=1, source_target_pairs={{0,1},{1,0},{2,3},{3,2},{4,5},{5,4},{6,7},{7,6},{8,9},{9,8},{10,11... | collective-permute-start | bytes 3145736 | tf_op jit(solution)/shard_map/ppermute | solution.py:276
  0.5 1.2 %copy-start = (bf16[128,1,4096]{2,0,1:T(8,128)(2,1)S(1)}, bf16[128,1,4096]{2,0,1:T(8,128)(2,1)}, u32[]{:S(2)}) copy-start(bf16[128,1,4096]{2,0,1:T(8,128)(2,1)} %param.4) | copy-start | bytes 3145732
  1.7 15.2 %collective-permute-start = (bf16[2,32,4096]{2,1,0:T(8,128)(2,1)S(1)}, bf16[2,32,4096]{2,1,0:T(8,128)(2,1)S(1)}, u32[]{:S(2)}, u32[]{:S(2)}) collective-permute-start(bf16[2,32,4096]{2,1,0:T(8,128)(2,1)S(1)} %picked_rows.3), channel_id=1, source_target_pairs={{0,2},{1,3},{2,0},{3,1},{4,6},{5,7},{6,4},{7,5},{8,10},{9,11},{10,... | collective-permute-start | bytes 1572872 | tf_op jit(solution)/shard_map/ppermute | solution.py:276
  4.3 6.0 %copy-start.1 = (bf16[128,1,4096]{2,0,1:T(8,128)(2,1)S(1)}, bf16[128,1,4096]{2,0,1:T(8,128)(2,1)}, u32[]{:S(2)}) copy-start(bf16[128,1,4096]{2,0,1:T(8,128)(2,1)} %param.4) | copy-start | bytes 3145732
  16.9 2.2 %collective-permute-start.2 = (bf16[2,32,4096]{2,1,0:T(8,128)(2,1)S(1)}, bf16[2,32,4096]{2,1,0:T(8,128)(2,1)S(1)}, u32[]{:S(2)}, u32[]{:S(2)}) collective-permute-start(bf16[2,32,4096]{2,1,0:T(8,128)(2,1)S(1)} %picked_rows.4), channel_id=1, source_target_pairs={{0,1},{1,0},{2,3},{3,2},{4,5},{5,4},{6,7},{7,6},{8,9},{9,8},{10,11... | collective-permute-start | bytes 1572872 | tf_op jit(solution)/shard_map/ppermute | solution.py:276
  17.3 25.6 %collective-permute-start.3 = (bf16[4,32,4096]{2,1,0:T(8,128)(2,1)S(1)}, bf16[4,32,4096]{2,1,0:T(8,128)(2,1)S(1)}, u32[]{:S(2)}, u32[]{:S(2)}) collective-permute-start(bf16[4,32,4096]{2,1,0:T(8,128)(2,1)S(1)} %picked_rows.5), channel_id=1, source_target_pairs={{0,2},{1,3},{2,0},{3,1},{4,6},{5,7},{6,4},{7,5},{8,10},{9,11},{10,... | collective-permute-start | bytes 3145736 | tf_op jit(solution)/shard_map/ppermute | solution.py:276
  22.7 25.6 %collective-permute-start.11 = (s16[33,16,128]{2,1,0:T(8,128)(2,1)S(1)}, s16[33,16,128]{2,1,0:T(8,128)(2,1)S(1)}, u32[]{:S(2)}, u32[]{:S(2)}) collective-permute-start(s16[33,16,128]{2,1,0:T(8,128)(2,1)S(1)} %get-tuple-element.30), channel_id=1, source_target_pairs={{0,16},{4,20},{8,24},{12,28},{16,0},{20,4},{24,8},{28,12},{1,17},{... | collective-permute-start | bytes 405512 | tf_op jit(solution)/shard_map/ppermute | solution.py:276
  25.5 24.5 %collective-permute-start.12 = (s16[33,16,128]{2,1,0:T(8,128)(2,1)S(1)}, s16[33,16,128]{2,1,0:T(8,128)(2,1)S(1)}, u32[]{:S(2)}, u32[]{:S(2)}) collective-permute-start(s16[33,16,128]{2,1,0:T(8,128)(2,1)S(1)} %get-tuple-element.31), channel_id=1, source_target_pairs={{0,20},{4,16},{8,28},{12,24},{16,4},{20,0},{24,12},{28,8},{1,21},{... | collective-permute-start | bytes 405512 | tf_op jit(solution)/shard_map/ppermute | solution.py:276
  26.7 23.4 %collective-permute-start.13 = (s16[33,16,128]{2,1,0:T(8,128)(2,1)S(1)}, s16[33,16,128]{2,1,0:T(8,128)(2,1)S(1)}, u32[]{:S(2)}, u32[]{:S(2)}) collective-permute-start(s16[33,16,128]{2,1,0:T(8,128)(2,1)S(1)} %get-tuple-element.32), channel_id=1, source_target_pairs={{0,24},{4,28},{8,16},{12,20},{16,8},{20,12},{24,0},{28,4},{1,25},{... | collective-permute-start | bytes 405512 | tf_op jit(solution)/shard_map/ppermute | solution.py:276
  30.3 22.6 %collective-permute-start.14 = (s16[33,16,128]{2,1,0:T(8,128)(2,1)S(1)}, s16[33,16,128]{2,1,0:T(8,128)(2,1)S(1)}, u32[]{:S(2)}, u32[]{:S(2)}) collective-permute-start(s16[33,16,128]{2,1,0:T(8,128)(2,1)S(1)} %get-tuple-element.33), channel_id=1, source_target_pairs={{0,28},{4,24},{8,20},{12,16},{16,12},{20,8},{24,4},{28,0},{1,29},{... | collective-permute-start | bytes 405512 | tf_op jit(solution)/shard_map/ppermute | solution.py:276
  42.9 24.9 %copy-start.3 = (s32[8,2]{0,1:T(2,128)S(1)}, s32[8,2]{0,1:T(2,128)}, u32[]{:S(2)}) copy-start(s32[8,2]{0,1:T(2,128)} %param.6) | copy-start | bytes 196
  42.9 25.1 %copy-start.2 = (s32[8]{0:T(128)S(1)}, s32[8]{0:T(128)}, u32[]{:S(2)}) copy-start(s32[8]{0:T(128)} %counts.5) | copy-start | bytes 100
  42.9 11.6 %collective-permute-start.15 = (s16[33,16,128]{2,1,0:T(8,128)(2,1)S(1)}, s16[33,16,128]{2,1,0:T(8,128)(2,1)S(1)}, u32[]{:S(2)}, u32[]{:S(2)}) collective-permute-start(s16[33,16,128]{2,1,0:T(8,128)(2,1)S(1)} %get-tuple-element.34), channel_id=1, source_target_pairs={{0,4},{4,0},{8,12},{12,8},{16,20},{20,16},{24,28},{28,24},{1,5},{5... | collective-permute-start | bytes 405512 | tf_op jit(solution)/shard_map/ppermute | solution.py:276
  48.3 11.3 %collective-permute-start.16 = (s16[33,16,128]{2,1,0:T(8,128)(2,1)S(1)}, s16[33,16,128]{2,1,0:T(8,128)(2,1)S(1)}, u32[]{:S(2)}, u32[]{:S(2)}) collective-permute-start(s16[33,16,128]{2,1,0:T(8,128)(2,1)S(1)} %get-tuple-element.35), channel_id=1, source_target_pairs={{0,8},{4,12},{8,0},{12,4},{16,24},{20,28},{24,16},{28,20},{1,9},{5... | collective-permute-start | bytes 405512 | tf_op jit(solution)/shard_map/ppermute | solution.py:276
  50.0 10.8 %collective-permute-start.17 = (s16[33,16,128]{2,1,0:T(8,128)(2,1)S(1)}, s16[33,16,128]{2,1,0:T(8,128)(2,1)S(1)}, u32[]{:S(2)}, u32[]{:S(2)}) collective-permute-start(s16[33,16,128]{2,1,0:T(8,128)(2,1)S(1)} %get-tuple-element.36), channel_id=1, source_target_pairs={{0,12},{4,8},{8,4},{12,0},{16,28},{20,24},{24,20},{28,16},{1,13},{... | collective-permute-start | bytes 405512 | tf_op jit(solution)/shard_map/ppermute | solution.py:276
  50.1 13.3 %collective-permute-start.7 = (s16[33,16,128]{2,1,0:T(8,128)(2,1)S(1)}, s16[33,16,128]{2,1,0:T(8,128)(2,1)S(1)}, u32[]{:S(2)}, u32[]{:S(2)}) collective-permute-start(s16[33,16,128]{2,1,0:T(8,128)(2,1)S(1)} %get-tuple-element.25), channel_id=1, source_target_pairs={{0,16},{4,20},{8,24},{12,28},{16,0},{20,4},{24,8},{28,12},{1,17},{... | collective-permute-start | bytes 405512 | tf_op jit(solution)/shard_map/ppermute | solution.py:276
  52.9 14.9 %collective-permute-start.8 = (s16[33,16,128]{2,1,0:T(8,128)(2,1)S(1)}, s16[33,16,128]{2,1,0:T(8,128)(2,1)S(1)}, u32[]{:S(2)}, u32[]{:S(2)}) collective-permute-start(s16[33,16,128]{2,1,0:T(8,128)(2,1)S(1)} %get-tuple-element.26), channel_id=1, source_target_pairs={{0,4},{4,0},{8,12},{12,8},{16,20},{20,16},{24,28},{28,24},{1,5},{5... | collective-permute-start | bytes 405512 | tf_op jit(solution)/shard_map/ppermute | solution.py:276
  54.5 16.7 %collective-permute-start.9 = (s16[33,16,128]{2,1,0:T(8,128)(2,1)S(1)}, s16[33,16,128]{2,1,0:T(8,128)(2,1)S(1)}, u32[]{:S(2)}, u32[]{:S(2)}) collective-permute-start(s16[33,16,128]{2,1,0:T(8,128)(2,1)S(1)} %get-tuple-element.27), channel_id=1, source_target_pairs={{0,20},{4,16},{8,28},{12,24},{16,4},{20,0},{24,12},{28,8},{1,21},{... | collective-permute-start | bytes 405512 | tf_op jit(solution)/shard_map/ppermute | solution.py:276
  59.6 11.6 %collective-permute-start.10 = (s16[33,16,128]{2,1,0:T(8,128)(2,1)S(1)}, s16[33,16,128]{2,1,0:T(8,128)(2,1)S(1)}, u32[]{:S(2)}, u32[]{:S(2)}) collective-permute-start(s16[33,16,128]{2,1,0:T(8,128)(2,1)S(1)} %get-tuple-element.28), channel_id=1, source_target_pairs={{0,8},{4,12},{8,0},{12,4},{16,24},{20,28},{24,16},{28,20},{1,9},{5... | collective-permute-start | bytes 405512 | tf_op jit(solution)/shard_map/ppermute | solution.py:276
  60.8 11.6 %collective-permute-start.4 = (s16[33,16,128]{2,1,0:T(8,128)(2,1)S(1)}, s16[33,16,128]{2,1,0:T(8,128)(2,1)S(1)}, u32[]{:S(2)}, u32[]{:S(2)}) collective-permute-start(s16[33,16,128]{2,1,0:T(8,128)(2,1)S(1)} %get-tuple-element.22), channel_id=1, source_target_pairs={{0,24},{4,28},{8,16},{12,20},{16,8},{20,12},{24,0},{28,4},{1,25},{... | collective-permute-start | bytes 405512 | tf_op jit(solution)/shard_map/ppermute | solution.py:276
  63.4 10.9 %collective-permute-start.5 = (s16[33,16,128]{2,1,0:T(8,128)(2,1)S(1)}, s16[33,16,128]{2,1,0:T(8,128)(2,1)S(1)}, u32[]{:S(2)}, u32[]{:S(2)}) collective-permute-start(s16[33,16,128]{2,1,0:T(8,128)(2,1)S(1)} %get-tuple-element.23), channel_id=1, source_target_pairs={{0,28},{4,24},{8,20},{12,16},{16,12},{20,8},{24,4},{28,0},{1,29},{... | collective-permute-start | bytes 405512 | tf_op jit(solution)/shard_map/ppermute | solution.py:276
  67.8 7.6 %collective-permute-start.6 = (s16[33,16,128]{2,1,0:T(8,128)(2,1)S(1)}, s16[33,16,128]{2,1,0:T(8,128)(2,1)S(1)}, u32[]{:S(2)}, u32[]{:S(2)}) collective-permute-start(s16[33,16,128]{2,1,0:T(8,128)(2,1)S(1)} %get-tuple-element.24), channel_id=1, source_target_pairs={{0,12},{4,8},{8,4},{12,0},{16,28},{20,24},{24,20},{28,16},{1,13},{... | collective-permute-start | bytes 405512 | tf_op jit(solution)/shard_map/ppermute | solution.py:276

commit v4 on v3

--- a/solution.py
+++ b/solution.py
@@ -46,13 +46,12 @@
     lane = lax.broadcasted_iota(jnp.int32, (16, 128), 1)
 
     def one_slot(slot, codes):
-        multiply(slot)
         codes = list(codes)
         for b in range(blocks):
             first = b * height
             for c, rows in enumerate(parts):
                 for g in range(rows // 16):
-                    value = total[first : first + 16, :]
+                    value = total[slot, first : first + 16, :]
                     first += 16
                     peak = jnp.max(jnp.abs(value), axis=1, keepdims=True)
                     exponent, mantissa = scale_code(peak)
@@ -67,8 +66,12 @@
                     codes[b * len(parts) + c] = jnp.where(lane == spot + 1, mantissa.astype(jnp.int32), code)
         return tuple(codes)
 
-    empty = tuple(jnp.zeros((16, 128), jnp.int32) for _ in range(blocks * len(parts)))
-    codes = lax.fori_loop(0, slots, one_slot, empty)
+    codes = tuple(jnp.zeros((16, 128), jnp.int32) for _ in range(blocks * len(parts)))
+    multiply(0)
+    for slot in range(slots):
+        if slot + 1 < slots:
+            multiply(slot + 1)
+        codes = one_slot(slot, codes)
     for b in range(blocks):
         for c, rows in enumerate(parts):
             put(c, b, slots * (rows // 16) * lanes, codes[b * len(parts) + c].astype(jnp.int16))
@@ -96,7 +99,7 @@
     def multiply(slot):
         for n in range(0, kept.shape[3], 256):
             wide = slice(n, n + 256)
-            total[:, wide] = jnp.dot(left[...], kept[0, slot, :, wide], preferred_element_type=jnp.float32)
+            total[slot, :, wide] = jnp.dot(left[...], kept[0, slot, :, wide], preferred_element_type=jnp.float32)
 
     return multiply
 
@@ -155,7 +158,7 @@
         out_specs=vmem,
         scratch_shapes=[
             pltpu.VMEM((2 * share * rows, depth), integrals.dtype),
-            pltpu.VMEM((2 * share * rows, cols), jnp.float32),
+            pltpu.VMEM((slots, 2 * share * rows, cols), jnp.float32),
         ],
         compiler_params=pltpu.CompilerParams(vmem_limit_bytes=16 * MIB),
         cost_estimate=pl.CostEstimate(
@@ -182,7 +185,7 @@
         out_specs=[vmem] * wide,
         scratch_shapes=[
             pltpu.VMEM((blocks * rows, depth), integrals.dtype),
-            pltpu.VMEM((blocks * rows, cols), jnp.float32),
+            pltpu.VMEM((slots, blocks * rows, cols), jnp.float32),
             pltpu.VMEM((wide, tiles, 16, 128), jnp.int16),
         ],
         compiler_params=pltpu.CompilerParams(vmem_limit_bytes=16 * MIB),

time: 77.7 us -> 77.7 us (level)
  Pallas kernels: 25.2 us -> 24 us
  transfers between devices with their start and end apart: 18 -> 18, of which waited for: 7 -> 7; matrix products, arithmetic and copies ran while one was open for 1% -> 1% of each run, Pallas kernels for 30% -> 28%
where the time goes in v4:
time: 77.7 us; the launch traced here: 77.5 us
  starting transfers between devices  28.2 us (36%)
  Pallas kernels  24 us (31%)
  waiting for transfers between devices  23.1 us (30%)
  local copies, waits for them, and re-layouts  1.67 us (2%)
    ppermute x18, starting transfers between devices, across(): return lax.ppermute(array, axis, [(i, i ^ bits) for i in range(size)])  28.2 us
    ppermute x18, waiting for transfers between devices, across(): return lax.ppermute(array, axis, [(i, i ^ bits) for i in range(size)])  23.1 us
    pallas_call x2, Pallas kernels, far_products(): pl.pallas_call(functools.partial(far_kernel, slots, wide, count, share, r...  6.67 us
    pallas_call x1, Pallas kernels, staged(): pl.pallas_call(stage_kernel, out_shape=pltpu.VMEM(integrals.shape, integr...  5.87 us
    pallas_call x3, Pallas kernels, summed(): pl.pallas_call(functools.partial(sum_kernel, slots, plan, start, rows, co...  5.83 us
    pallas_call x2, Pallas kernels, near_products(): pl.pallas_call(functools.partial(near_kernel, slots, share, len(after)),...  5.32 us
  transfers between devices with their start and end apart: 18, of which 7 were waited for; matrix products, arithmetic and copies ran while one was open for 1% of the time, Pallas kernels for 28%

profile of v4, /device:TPU:0, one launch (start us, length us, event | category | flops | bytes accessed | tf_op | source)
XLA Modules:
  0.0 77.5 jit_solution(16528901933791775988)
XLA Ops:
  0.0 0.5 collective-permute-start.1
  0.5 1.2 %copy-done = bf16[128,1,4096]{2,0,1:T(8,128)(2,1)S(1)} copy-done((bf16[128,1,4096]{2,0,1:T(8,128)(2,1)S(1)}, bf16[128,1,4096]{2,0,1:T(8,128)(2,1)}, u32[]{:S(2)}) %copy-start) | copy-done | bytes 1048600
  1.7 2.6 %collective-permute-start = (bf16[2,32,4096]{2,1,0:T(8,128)(2,1)S(1)}, bf16[2,32,4096]{2,1,0:T(8,128)(2,1)S(1)}, u32[]{:S(2)}, u32[]{:S(2)}) collective-permute-start(bf16[2,32,4096]{2,1,0:T(8,128)(2,1)S(1)} %picked_rows.3), channel_id=1, source_target_pairs={{0,2},{1,3},{2,0},{3,1},{4,6},{5,7},{6,4},{7,5},{8,10},{9,11},{10,... | collective-permute-start | bytes 1572872 | tf_op jit(solution)/shard_map/ppermute | solution.py:279
  4.3 5.9 %staged_integrals.1.refs_2_.refs_0_.refs_3_ = bf16[1,2,4096,1024]{3,2,1,0:T(8,128)(2,1)S(1)} custom-call(bf16[1,2,4096,1024]{3,2,1,0:T(8,128)(2,1)} %source.1), custom_call_target="tpu_custom_call" | custom-call | tf_op jit(solution)/shard_map/staged_integrals/pallas_call | solution.py:87
  10.5 2.7 %near_products.2.refs_1_.refs_2_ = s16[4,33,16,128]{3,2,1,0:T(8,128)(2,1)S(1)} custom-call(bf16[2,32,4096]{2,1,0:T(8,128)(2,1)S(1)} %get-tuple-element.38.refs_0_, bf16[2,32,4096]{2,1,0:T(8,128)(2,1)S(1)} %get-tuple-element.40.refs_1_, bf16[1,2,4096,1024]{3,2,1,0:T(8,128)(2,1)S(1)} %staged_integrals.1.refs_2_.refs_0_.refs_3_), custom_call_target="tpu_custom_call" | custom-call | flops 17179869184 | bytes 1048576 | tf_op jit(solution)/shard_map/near_products/pallas_call | solution.py:154
  13.1 3.8 %collective-permute-done.source.refs_0_ = bf16[2,32,4096]{2,1,0:T(8,128)(2,1)S(1)} collective-permute-done((bf16[2,32,4096]{2,1,0:T(8,128)(2,1)S(1)}, bf16[2,32,4096]{2,1,0:T(8,128)(2,1)S(1)}, u32[]{:S(2)}, u32[]{:S(2)}) %collective-permute-start) | collective-permute-done | bytes 524320 | tf_op jit(solution)/shard_map/ppermute | solution.py:279
  17.2 0.3 picked_rows.5
  17.5 1.8 %collective-permute-start.3 = (bf16[4,32,4096]{2,1,0:T(8,128)(2,1)S(1)}, bf16[4,32,4096]{2,1,0:T(8,128)(2,1)S(1)}, u32[]{:S(2)}, u32[]{:S(2)}) collective-permute-start(bf16[4,32,4096]{2,1,0:T(8,128)(2,1)S(1)} %picked_rows.5), channel_id=1, source_target_pairs={{0,2},{1,3},{2,0},{3,1},{4,6},{5,7},{6,4},{7,5},{8,10},{9,11},{10,... | collective-permute-start | bytes 3145736 | tf_op jit(solution)/shard_map/ppermute | solution.py:279
  19.3 3.3 %far_products.2 = (s16[33,16,128]{2,1,0:T(8,128)(2,1)S(1)}, s16[33,16,128]{2,1,0:T(8,128)(2,1)S(1)}, s16[33,16,128]{2,1,0:T(8,128)(2,1)S(1)}, s16[33,16,128]{2,1...) custom-call(s32[2]{0:T(128)S(1)} %pad_add_fusion.ids, ...), custom_call_target="tpu_custom_call" | custom-call | flops 17179869184 | bytes 1048576 | tf_op jit(solution)/shard_map/far_products/pallas_call | solution.py:179
  22.6 2.6 %collective-permute-start.11 = (s16[33,16,128]{2,1,0:T(8,128)(2,1)S(1)}, s16[33,16,128]{2,1,0:T(8,128)(2,1)S(1)}, u32[]{:S(2)}, u32[]{:S(2)}) collective-permute-start(s16[33,16,128]{2,1,0:T(8,128)(2,1)S(1)} %get-tuple-element.30), channel_id=1, source_target_pairs={{0,16},{4,20},{8,24},{12,28},{16,0},{20,4},{24,8},{28,12},{1,17},{... | collective-permute-start | bytes 405512 | tf_op jit(solution)/shard_map/ppermute | solution.py:279
  25.2 1.3 %collective-permute-start.12 = (s16[33,16,128]{2,1,0:T(8,128)(2,1)S(1)}, s16[33,16,128]{2,1,0:T(8,128)(2,1)S(1)}, u32[]{:S(2)}, u32[]{:S(2)}) collective-permute-start(s16[33,16,128]{2,1,0:T(8,128)(2,1)S(1)} %get-tuple-element.31), channel_id=1, source_target_pairs={{0,20},{4,16},{8,28},{12,24},{16,4},{20,0},{24,12},{28,8},{1,21},{... | collective-permute-start | bytes 405512 | tf_op jit(solution)/shard_map/ppermute | solution.py:279
  26.5 3.6 %collective-permute-start.13 = (s16[33,16,128]{2,1,0:T(8,128)(2,1)S(1)}, s16[33,16,128]{2,1,0:T(8,128)(2,1)S(1)}, u32[]{:S(2)}, u32[]{:S(2)}) collective-permute-start(s16[33,16,128]{2,1,0:T(8,128)(2,1)S(1)} %get-tuple-element.32), channel_id=1, source_target_pairs={{0,24},{4,28},{8,16},{12,20},{16,8},{20,12},{24,0},{28,4},{1,25},{... | collective-permute-start | bytes 405512 | tf_op jit(solution)/shard_map/ppermute | solution.py:279
  30.1 0.2 collective-permute-start.14
  30.3 2.7 %near_products.3.refs_2_ = s16[4,33,16,128]{3,2,1,0:T(8,128)(2,1)S(1)} custom-call(s16[33,16,128]{2,1,0:T(8,128)(2,1)S(1)} %get-tuple-element.21.refs_0_.refs_7_, bf16[2,32,4096]{2,1,0:T(8,128)(2,1)S(1)} %get-tuple-element.37.refs_1_, bf16[2,32,4096]{2,1,0:T(8,128)(2,1)S(1)} %get-tuple-element.39.refs_2_, ...), custom_call_target="tpu_custom_call" | custom-call | flops 17179869184 | bytes 1048576 | tf_op jit(solution)/shard_map/near_products/pallas_call | solution.py:154
  33.0 10.1 %collective-permute-done.3.refs_1_ = bf16[4,32,4096]{2,1,0:T(8,128)(2,1)S(1)} collective-permute-done((bf16[4,32,4096]{2,1,0:T(8,128)(2,1)S(1)}, bf16[4,32,4096]{2,1,0:T(8,128)(2,1)S(1)}, u32[]{:S(2)}, u32[]{:S(2)}) %collective-permute-start.3) | collective-permute-done | bytes 1048608 | tf_op jit(solution)/shard_map/ppermute | solution.py:279
  43.1 1.8 %collective-permute-start.15 = (s16[33,16,128]{2,1,0:T(8,128)(2,1)S(1)}, s16[33,16,128]{2,1,0:T(8,128)(2,1)S(1)}, u32[]{:S(2)}, u32[]{:S(2)}) collective-permute-start(s16[33,16,128]{2,1,0:T(8,128)(2,1)S(1)} %get-tuple-element.34), channel_id=1, source_target_pairs={{0,4},{4,0},{8,12},{12,8},{16,20},{20,16},{24,28},{28,24},{1,5},{5... | collective-permute-start | bytes 405512 | tf_op jit(solution)/shard_map/ppermute | solution.py:279
  44.9 3.4 %far_products.3 = (s16[33,16,128]{2,1,0:T(8,128)(2,1)S(1)}, s16[33,16,128]{2,1,0:T(8,128)(2,1)S(1)}, s16[33,16,128]{2,1,0:T(8,128)(2,1)S(1)}, s16[33,16,128]{2,1...) custom-call(s32[2]{0:T(128)S(1)} %pad_add_fusion.ids, ...), custom_call_target="tpu_custom_call" | custom-call | flops 17179869184 | bytes 1048576 | tf_op jit(solution)/shard_map/far_products/pallas_call | solution.py:179
  48.2 1.6 %collective-permute-start.16 = (s16[33,16,128]{2,1,0:T(8,128)(2,1)S(1)}, s16[33,16,128]{2,1,0:T(8,128)(2,1)S(1)}, u32[]{:S(2)}, u32[]{:S(2)}) collective-permute-start(s16[33,16,128]{2,1,0:T(8,128)(2,1)S(1)} %get-tuple-element.35), channel_id=1, source_target_pairs={{0,8},{4,12},{8,0},{12,4},{16,24},{20,28},{24,16},{28,20},{1,9},{5... | collective-permute-start | bytes 405512 | tf_op jit(solution)/shard_map/ppermute | solution.py:279
  49.9 0.2 collective-permute-start.17
  50.0 2.8 %collective-permute-start.7 = (s16[33,16,128]{2,1,0:T(8,128)(2,1)S(1)}, s16[33,16,128]{2,1,0:T(8,128)(2,1)S(1)}, u32[]{:S(2)}, u32[]{:S(2)}) collective-permute-start(s16[33,16,128]{2,1,0:T(8,128)(2,1)S(1)} %get-tuple-element.25), channel_id=1, source_target_pairs={{0,16},{4,20},{8,24},{12,28},{16,0},{20,4},{24,8},{28,12},{1,17},{... | collective-permute-start | bytes 405512 | tf_op jit(solution)/shard_map/ppermute | solution.py:279
  52.9 1.5 %collective-permute-start.8 = (s16[33,16,128]{2,1,0:T(8,128)(2,1)S(1)}, s16[33,16,128]{2,1,0:T(8,128)(2,1)S(1)}, u32[]{:S(2)}, u32[]{:S(2)}) collective-permute-start(s16[33,16,128]{2,1,0:T(8,128)(2,1)S(1)} %get-tuple-element.26), channel_id=1, source_target_pairs={{0,4},{4,0},{8,12},{12,8},{16,20},{20,16},{24,28},{28,24},{1,5},{5... | collective-permute-start | bytes 405512 | tf_op jit(solution)/shard_map/ppermute | solution.py:279
  54.4 0.6 collective-permute-start.9
  55.0 4.5 %collective-permute-done.16.refs_5_ = s16[33,16,128]{2,1,0:T(8,128)(2,1)S(1)} collective-permute-done((s16[33,16,128]{2,1,0:T(8,128)(2,1)S(1)}, s16[33,16,128]{2,1,0:T(8,128)(2,1)S(1)}, u32[]{:S(2)}, u32[]{:S(2)}) %collective-permute-start.16) | collective-permute-done | bytes 135200 | tf_op jit(solution)/shard_map/ppermute | solution.py:279
  59.5 1.1 %collective-permute-done.17.refs_6_ = s16[33,16,128]{2,1,0:T(8,128)(2,1)S(1)} collective-permute-done((s16[33,16,128]{2,1,0:T(8,128)(2,1)S(1)}, s16[33,16,128]{2,1,0:T(8,128)(2,1)S(1)}, u32[]{:S(2)}, u32[]{:S(2)}) %collective-permute-start.17) | collective-permute-done | bytes 135200 | tf_op jit(solution)/shard_map/ppermute | solution.py:279
  60.7 2.7 %collective-permute-start.4 = (s16[33,16,128]{2,1,0:T(8,128)(2,1)S(1)}, s16[33,16,128]{2,1,0:T(8,128)(2,1)S(1)}, u32[]{:S(2)}, u32[]{:S(2)}) collective-permute-start(s16[33,16,128]{2,1,0:T(8,128)(2,1)S(1)} %get-tuple-element.22), channel_id=1, source_target_pairs={{0,24},{4,28},{8,16},{12,20},{16,8},{20,12},{24,0},{28,4},{1,25},{... | collective-permute-start | bytes 405512 | tf_op jit(solution)/shard_map/ppermute | solution.py:279
  63.4 4.4 %collective-permute-start.5 = (s16[33,16,128]{2,1,0:T(8,128)(2,1)S(1)}, s16[33,16,128]{2,1,0:T(8,128)(2,1)S(1)}, u32[]{:S(2)}, u32[]{:S(2)}) collective-permute-start(s16[33,16,128]{2,1,0:T(8,128)(2,1)S(1)} %get-tuple-element.23), channel_id=1, source_target_pairs={{0,28},{4,24},{8,20},{12,16},{16,12},{20,8},{24,4},{28,0},{1,29},{... | collective-permute-start | bytes 405512 | tf_op jit(solution)/shard_map/ppermute | solution.py:279
  67.9 2.6 %tile_sums.4.refs_4_ = f32[64,8,1024]{2,1,0:T(8,128)} custom-call(s32[2]{0:T(128)S(1)} %pad_add_fusion.ids, s32[16]{0:T(128)S(1)} %reshape.8.targets, s32[8]{0:T(128)S(1)} %copy-done.2, s16[33,16,128]{2,1,0:T(8,128)(2,1)S(1)} %collective-permute-done.11.refs_0_, s16[33,16,128]{2,1,0:T(8,128)(2,1)S(1)} %collective-permute-done.12.refs_1_, ...), custom_call_target="tpu_custom_call" | custom-call | flops 2097152 | bytes 2097152 | tf_op jit(solution)/shard_map/tile_sums/pallas_call | solution.py:251
  70.5 0.6 collective-permute-done.9.refs_2_
  71.1 1.2 %tile_sums.3.refs_3_ = f32[8,32,1024]{2,1,0:T(8,128)S(1)} custom-call(s32[2]{0:T(128)S(1)} %pad_add_fusion.ids, s32[16]{0:T(128)S(1)} %reshape.8.targets, s32[8]{0:T(128)S(1)} %copy-done.2, s16[33,16,128]{2,1,0:T(8,128)(2,1)S(1)} %collective-permute-done.7.refs_0_, s16[33,16,128]{2,1,0:T(8,128)(2,1)S(1)} %collective-permute-done.8.refs_1_, ...), custom_call_target="tpu_custom_call" | custom-call | flops 1310720 | bytes 1703936 | tf_op jit(solution)/shard_map/tile_sums/pallas_call | solution.py:251
  72.3 1.9 %collective-permute-done.5.refs_1_ = s16[33,16,128]{2,1,0:T(8,128)(2,1)S(1)} collective-permute-done((s16[33,16,128]{2,1,0:T(8,128)(2,1)S(1)}, s16[33,16,128]{2,1,0:T(8,128)(2,1)S(1)}, u32[]{:S(2)}, u32[]{:S(2)}) %collective-permute-start.5) | collective-permute-done | bytes 135200 | tf_op jit(solution)/shard_map/ppermute | solution.py:279
  74.2 1.1 %collective-permute-done.6.refs_2_ = s16[33,16,128]{2,1,0:T(8,128)(2,1)S(1)} collective-permute-done((s16[33,16,128]{2,1,0:T(8,128)(2,1)S(1)}, s16[33,16,128]{2,1,0:T(8,128)(2,1)S(1)}, u32[]{:S(2)}, u32[]{:S(2)}) %collective-permute-start.6) | collective-permute-done | bytes 135200 | tf_op jit(solution)/shard_map/ppermute | solution.py:279
  75.3 2.0 %tile_sums.5 = f32[64,8,1024]{2,1,0:T(8,128)} custom-call(s32[2]{0:T(128)S(1)} %pad_add_fusion.ids, s32[16]{0:T(128)S(1)} %reshape.8.targets, s32[8]{0:T(128)S(1)} %copy-done.2, s16[33,16,128]{2,1,0:T(8,128)(2,1)S(1)} %collective-permute-done.4.refs_0_, s16[33,16,128]{2,1,0:T(8,128)(2,1)S(1)} %collective-permute-done.5.refs_1_, ...), custom_call_target="tpu_custom_call", output_to_operand_aliasing={{}: (7, {})} | custom-call | flops 786432 | bytes 1441792 | tf_op jit(solution)/shard_map/tile_sums/pallas_call | solution.py:251
  (29 shorter events, 0.8 us)
Async XLA Ops:
  0.0 10.4 %collective-permute-start.1 = (bf16[2,64,4096]{2,1,0:T(8,128)(2,1)}, bf16[2,64,4096]{2,1,0:T(8,128)(2,1)S(1)}, u32[]{:S(2)}, u32[]{:S(2)}) collective-permute-start(bf16[2,64,4096]{2,1,0:T(8,128)(2,1)} %bitcast.3), channel_id=1, source_target_pairs={{0,1},{1,0},{2,3},{3,2},{4,5},{5,4},{6,7},{7,6},{8,9},{9,8},{10,11... | collective-permute-start | bytes 3145736 | tf_op jit(solution)/shard_map/ppermute | solution.py:279
  0.5 1.2 %copy-start = (bf16[128,1,4096]{2,0,1:T(8,128)(2,1)S(1)}, bf16[128,1,4096]{2,0,1:T(8,128)(2,1)}, u32[]{:S(2)}) copy-start(bf16[128,1,4096]{2,0,1:T(8,128)(2,1)} %param.4) | copy-start | bytes 3145732
  1.7 15.2 %collective-permute-start = (bf16[2,32,4096]{2,1,0:T(8,128)(2,1)S(1)}, bf16[2,32,4096]{2,1,0:T(8,128)(2,1)S(1)}, u32[]{:S(2)}, u32[]{:S(2)}) collective-permute-start(bf16[2,32,4096]{2,1,0:T(8,128)(2,1)S(1)} %picked_rows.3), channel_id=1, source_target_pairs={{0,2},{1,3},{2,0},{3,1},{4,6},{5,7},{6,4},{7,5},{8,10},{9,11},{10,... | collective-permute-start | bytes 1572872 | tf_op jit(solution)/shard_map/ppermute | solution.py:279
  4.3 6.0 %copy-start.1 = (bf16[128,1,4096]{2,0,1:T(8,128)(2,1)S(1)}, bf16[128,1,4096]{2,0,1:T(8,128)(2,1)}, u32[]{:S(2)}) copy-start(bf16[128,1,4096]{2,0,1:T(8,128)(2,1)} %param.4) | copy-start | bytes 3145732
  16.9 2.3 %collective-permute-start.2 = (bf16[2,32,4096]{2,1,0:T(8,128)(2,1)S(1)}, bf16[2,32,4096]{2,1,0:T(8,128)(2,1)S(1)}, u32[]{:S(2)}, u32[]{:S(2)}) collective-permute-start(bf16[2,32,4096]{2,1,0:T(8,128)(2,1)S(1)} %picked_rows.4), channel_id=1, source_target_pairs={{0,1},{1,0},{2,3},{3,2},{4,5},{5,4},{6,7},{7,6},{8,9},{9,8},{10,11... | collective-permute-start | bytes 1572872 | tf_op jit(solution)/shard_map/ppermute | solution.py:279
  17.5 25.6 %collective-permute-start.3 = (bf16[4,32,4096]{2,1,0:T(8,128)(2,1)S(1)}, bf16[4,32,4096]{2,1,0:T(8,128)(2,1)S(1)}, u32[]{:S(2)}, u32[]{:S(2)}) collective-permute-start(bf16[4,32,4096]{2,1,0:T(8,128)(2,1)S(1)} %picked_rows.5), channel_id=1, source_target_pairs={{0,2},{1,3},{2,0},{3,1},{4,6},{5,7},{6,4},{7,5},{8,10},{9,11},{10,... | collective-permute-start | bytes 3145736 | tf_op jit(solution)/shard_map/ppermute | solution.py:279
  22.6 25.6 %collective-permute-start.11 = (s16[33,16,128]{2,1,0:T(8,128)(2,1)S(1)}, s16[33,16,128]{2,1,0:T(8,128)(2,1)S(1)}, u32[]{:S(2)}, u32[]{:S(2)}) collective-permute-start(s16[33,16,128]{2,1,0:T(8,128)(2,1)S(1)} %get-tuple-element.30), channel_id=1, source_target_pairs={{0,16},{4,20},{8,24},{12,28},{16,0},{20,4},{24,8},{28,12},{1,17},{... | collective-permute-start | bytes 405512 | tf_op jit(solution)/shard_map/ppermute | solution.py:279
  25.2 24.6 %collective-permute-start.12 = (s16[33,16,128]{2,1,0:T(8,128)(2,1)S(1)}, s16[33,16,128]{2,1,0:T(8,128)(2,1)S(1)}, u32[]{:S(2)}, u32[]{:S(2)}) collective-permute-start(s16[33,16,128]{2,1,0:T(8,128)(2,1)S(1)} %get-tuple-element.31), channel_id=1, source_target_pairs={{0,20},{4,16},{8,28},{12,24},{16,4},{20,0},{24,12},{28,8},{1,21},{... | collective-permute-start | bytes 405512 | tf_op jit(solution)/shard_map/ppermute | solution.py:279
  26.5 23.5 %collective-permute-start.13 = (s16[33,16,128]{2,1,0:T(8,128)(2,1)S(1)}, s16[33,16,128]{2,1,0:T(8,128)(2,1)S(1)}, u32[]{:S(2)}, u32[]{:S(2)}) collective-permute-start(s16[33,16,128]{2,1,0:T(8,128)(2,1)S(1)} %get-tuple-element.32), channel_id=1, source_target_pairs={{0,24},{4,28},{8,16},{12,20},{16,8},{20,12},{24,0},{28,4},{1,25},{... | collective-permute-start | bytes 405512 | tf_op jit(solution)/shard_map/ppermute | solution.py:279
  30.1 22.7 %collective-permute-start.14 = (s16[33,16,128]{2,1,0:T(8,128)(2,1)S(1)}, s16[33,16,128]{2,1,0:T(8,128)(2,1)S(1)}, u32[]{:S(2)}, u32[]{:S(2)}) collective-permute-start(s16[33,16,128]{2,1,0:T(8,128)(2,1)S(1)} %get-tuple-element.33), channel_id=1, source_target_pairs={{0,28},{4,24},{8,20},{12,16},{16,12},{20,8},{24,4},{28,0},{1,29},{... | collective-permute-start | bytes 405512 | tf_op jit(solution)/shard_map/ppermute | solution.py:279
  43.1 24.6 %copy-start.3 = (s32[8,2]{0,1:T(2,128)S(1)}, s32[8,2]{0,1:T(2,128)}, u32[]{:S(2)}) copy-start(s32[8,2]{0,1:T(2,128)} %param.6) | copy-start | bytes 196
  43.1 24.8 %copy-start.2 = (s32[8]{0:T(128)S(1)}, s32[8]{0:T(128)}, u32[]{:S(2)}) copy-start(s32[8]{0:T(128)} %counts.5) | copy-start | bytes 100
  43.1 11.3 %collective-permute-start.15 = (s16[33,16,128]{2,1,0:T(8,128)(2,1)S(1)}, s16[33,16,128]{2,1,0:T(8,128)(2,1)S(1)}, u32[]{:S(2)}, u32[]{:S(2)}) collective-permute-start(s16[33,16,128]{2,1,0:T(8,128)(2,1)S(1)} %get-tuple-element.34), channel_id=1, source_target_pairs={{0,4},{4,0},{8,12},{12,8},{16,20},{20,16},{24,28},{28,24},{1,5},{5... | collective-permute-start | bytes 405512 | tf_op jit(solution)/shard_map/ppermute | solution.py:279
  48.2 11.3 %collective-permute-start.16 = (s16[33,16,128]{2,1,0:T(8,128)(2,1)S(1)}, s16[33,16,128]{2,1,0:T(8,128)(2,1)S(1)}, u32[]{:S(2)}, u32[]{:S(2)}) collective-permute-start(s16[33,16,128]{2,1,0:T(8,128)(2,1)S(1)} %get-tuple-element.35), channel_id=1, source_target_pairs={{0,8},{4,12},{8,0},{12,4},{16,24},{20,28},{24,16},{28,20},{1,9},{5... | collective-permute-start | bytes 405512 | tf_op jit(solution)/shard_map/ppermute | solution.py:279
  49.9 10.8 %collective-permute-start.17 = (s16[33,16,128]{2,1,0:T(8,128)(2,1)S(1)}, s16[33,16,128]{2,1,0:T(8,128)(2,1)S(1)}, u32[]{:S(2)}, u32[]{:S(2)}) collective-permute-start(s16[33,16,128]{2,1,0:T(8,128)(2,1)S(1)} %get-tuple-element.36), channel_id=1, source_target_pairs={{0,12},{4,8},{8,4},{12,0},{16,28},{20,24},{24,20},{28,16},{1,13},{... | collective-permute-start | bytes 405512 | tf_op jit(solution)/shard_map/ppermute | solution.py:279
  50.0 13.4 %collective-permute-start.7 = (s16[33,16,128]{2,1,0:T(8,128)(2,1)S(1)}, s16[33,16,128]{2,1,0:T(8,128)(2,1)S(1)}, u32[]{:S(2)}, u32[]{:S(2)}) collective-permute-start(s16[33,16,128]{2,1,0:T(8,128)(2,1)S(1)} %get-tuple-element.25), channel_id=1, source_target_pairs={{0,16},{4,20},{8,24},{12,28},{16,0},{20,4},{24,8},{28,12},{1,17},{... | collective-permute-start | bytes 405512 | tf_op jit(solution)/shard_map/ppermute | solution.py:279
  52.9 14.9 %collective-permute-start.8 = (s16[33,16,128]{2,1,0:T(8,128)(2,1)S(1)}, s16[33,16,128]{2,1,0:T(8,128)(2,1)S(1)}, u32[]{:S(2)}, u32[]{:S(2)}) collective-permute-start(s16[33,16,128]{2,1,0:T(8,128)(2,1)S(1)} %get-tuple-element.26), channel_id=1, source_target_pairs={{0,4},{4,0},{8,12},{12,8},{16,20},{20,16},{24,28},{28,24},{1,5},{5... | collective-permute-start | bytes 405512 | tf_op jit(solution)/shard_map/ppermute | solution.py:279
  54.4 16.7 %collective-permute-start.9 = (s16[33,16,128]{2,1,0:T(8,128)(2,1)S(1)}, s16[33,16,128]{2,1,0:T(8,128)(2,1)S(1)}, u32[]{:S(2)}, u32[]{:S(2)}) collective-permute-start(s16[33,16,128]{2,1,0:T(8,128)(2,1)S(1)} %get-tuple-element.27), channel_id=1, source_target_pairs={{0,20},{4,16},{8,28},{12,24},{16,4},{20,0},{24,12},{28,8},{1,21},{... | collective-permute-start | bytes 405512 | tf_op jit(solution)/shard_map/ppermute | solution.py:279
  59.5 11.5 %collective-permute-start.10 = (s16[33,16,128]{2,1,0:T(8,128)(2,1)S(1)}, s16[33,16,128]{2,1,0:T(8,128)(2,1)S(1)}, u32[]{:S(2)}, u32[]{:S(2)}) collective-permute-start(s16[33,16,128]{2,1,0:T(8,128)(2,1)S(1)} %get-tuple-element.28), channel_id=1, source_target_pairs={{0,8},{4,12},{8,0},{12,4},{16,24},{20,28},{24,16},{28,20},{1,9},{5... | collective-permute-start | bytes 405512 | tf_op jit(solution)/shard_map/ppermute | solution.py:279
  60.7 11.6 %collective-permute-start.4 = (s16[33,16,128]{2,1,0:T(8,128)(2,1)S(1)}, s16[33,16,128]{2,1,0:T(8,128)(2,1)S(1)}, u32[]{:S(2)}, u32[]{:S(2)}) collective-permute-start(s16[33,16,128]{2,1,0:T(8,128)(2,1)S(1)} %get-tuple-element.22), channel_id=1, source_target_pairs={{0,24},{4,28},{8,16},{12,20},{16,8},{20,12},{24,0},{28,4},{1,25},{... | collective-permute-start | bytes 405512 | tf_op jit(solution)/shard_map/ppermute | solution.py:279
  63.4 10.9 %collective-permute-start.5 = (s16[33,16,128]{2,1,0:T(8,128)(2,1)S(1)}, s16[33,16,128]{2,1,0:T(8,128)(2,1)S(1)}, u32[]{:S(2)}, u32[]{:S(2)}) collective-permute-start(s16[33,16,128]{2,1,0:T(8,128)(2,1)S(1)} %get-tuple-element.23), channel_id=1, source_target_pairs={{0,28},{4,24},{8,20},{12,16},{16,12},{20,8},{24,4},{28,0},{1,29},{... | collective-permute-start | bytes 405512 | tf_op jit(solution)/shard_map/ppermute | solution.py:279
  67.7 7.6 %collective-permute-start.6 = (s16[33,16,128]{2,1,0:T(8,128)(2,1)S(1)}, s16[33,16,128]{2,1,0:T(8,128)(2,1)S(1)}, u32[]{:S(2)}, u32[]{:S(2)}) collective-permute-start(s16[33,16,128]{2,1,0:T(8,128)(2,1)S(1)} %get-tuple-element.24), channel_id=1, source_target_pairs={{0,12},{4,8},{8,4},{12,0},{16,28},{20,24},{24,20},{28,16},{1,13},{... | collective-permute-start | bytes 405512 | tf_op jit(solution)/shard_map/ppermute | solution.py:279
